TPU v7x, 32 devices: a whole 2x2x4 slice. The times are simulated.
32 devices in a mesh: head: 8 (over z, core), mlp: 4 (over y, x).
Axes of the slice: x: 2, y: 2, z: 4, core: 2. Of those that a mesh axis runs over, the one named last changes fastest.
Arguments:
- tokens: bfloat16 [4, 1024, 2048], P('mlp', 'head'), may hold values from -6 to 6
- out_grad: bfloat16 [4, 1024, 2048], P('mlp', 'head'), may hold values from -6 to 6
- seq_lengths: int32 [4, 6], P('mlp'), may hold values from 1 to 57, as said below
- norm_gain: bfloat16 [2048], replicated, may hold values from 0.5 to 1.5
- in_weight: bfloat16 [2048, 4, 2048], P(None, None, 'head'), may hold values from -0.125 to 0.125
- rate_weight: bfloat16 [2048, 32], P(None, 'head'), may hold values from -0.125 to 0.125
- init_state: bfloat16 [32, 64, 64], P('head'), may hold values from -0.75 to 0.75
- mix_gain: bfloat16 [2048], P('head'), may hold values from 0.5 to 1.5
- mix_bias: bfloat16 [2048], P('head'), may hold values from -1.5 to 1.5
- out_weight: bfloat16 [2048, 2048], P('head'), may hold values from -0.125 to 0.125
- mlp_gain: bfloat16 [2048], replicated, may hold values from 0.5 to 1.5
- gate_up: bfloat16 [2048, 2, 5504], P(None, None, 'mlp'), may hold values from -0.125 to 0.125
- down_weight: bfloat16 [5504, 2048], P('mlp'), may hold values from -0.078125 to 0.078125
Outputs:
- result: bfloat16 [4, 1024, 2048], P('mlp', 'head')
- grad_tokens: float32 [4, 1024, 2048], P('mlp', 'head')
- grad_norm_gain: float32 [2048], replicated
- grad_in_weight: float32 [2048, 4, 2048], P(None, None, 'head')
- grad_rate_weight: float32 [2048, 32], P(None, 'head')
- grad_init_state: float32 [32, 64, 64], P('head')
- grad_mix_gain: float32 [2048], P('head')
- grad_mix_bias: float32 [2048], P('head')
- grad_out_weight: float32 [2048, 2048], P('head')
- grad_mlp_gain: float32 [2048], replicated
- grad_gate_up: float32 [2048, 2, 5504], P(None, None, 'mlp')
- grad_down: float32 [5504, 2048], P('mlp')
Inputs may be any that keep to these rules, and one draw needn't show every extreme that they name: `seq_lengths`: each row holds the lengths of 6 sequences in steps of 16 tokens, packed in order; a row sums to 64; in every row one sequence has the largest length.
All inputs are finite; a program needn't handle non-finite values.
Results may differ from a plain program's by a relative error of at most 0.025.
Values may be sent and summed in bfloat16 or wider, within the bound.
A program may use at most 256 MiB of HBM per device.

v0:
```python
from functools import partial

import jax
import jax.numpy as jnp
from jax import lax
from jax.sharding import PartitionSpec as P

HEAD_DIM = 64
MINIBATCH = 16


PRECISE = lax.Precision.HIGHEST


def rms_scale(values):
    return lax.rsqrt(jnp.mean(values * values, axis=-1, keepdims=True) + 1e-06)


def norm_back(values, row_scale, gains, upstream):
    weighted = upstream * gains
    return row_scale * weighted - values * row_scale**3 * jnp.mean(
        weighted * values, axis=-1, keepdims=True
    )


def contract_rows(left, right):
    return lax.dot_general(
        left, right, (((0,), (0,)), ((), ())), preferred_element_type=jnp.float32
    )


def contract_cols(left, right):
    return lax.dot_general(
        left, right, (((1,), (1,)), ((), ())), preferred_element_type=jnp.float32
    )


def resets_of(lengths_row, block_count):
    end_marks = jnp.cumsum(lengths_row)
    starts = end_marks - lengths_row
    positions = jnp.arange(block_count, dtype=jnp.int32)
    return jnp.any(positions[:, None] == starts[None, :], axis=1).astype(jnp.float32)


def mixer(triple, gate_pre, rate_logit, initial, gains, biases, reset_flags):
    row_count = triple.shape[0]
    feature_width = triple.shape[2]
    head_count = feature_width // HEAD_DIM
    blocks = row_count // MINIBATCH
    split_rows = triple.reshape(blocks, MINIBATCH, 3, head_count, HEAD_DIM)
    step_rates = (jax.nn.sigmoid(rate_logit) / (MINIBATCH * HEAD_DIM)).reshape(
        blocks, MINIBATCH, head_count
    )
    positions = jnp.arange(MINIBATCH)
    causal = (positions[:, None] >= positions[None, :]).astype(jnp.float32)

    def advance(inner_state, scan_item):
        block_item, step_rate, reset_flag = scan_item
        inner_state = reset_flag * initial + (1.0 - reset_flag) * inner_state
        queries = block_item[:, 0]
        key_rows = block_item[:, 1]
        values = block_item[:, 2]
        residue = jnp.einsum("thi,hij->thj", key_rows, inner_state, precision=PRECISE) - values
        scores = jnp.einsum("thi,shi->hts", queries, key_rows, precision=PRECISE)
        scores = scores * causal[None] * step_rate.T[:, None, :]
        inner_out = jnp.einsum("thi,hij->thj", queries, inner_state, precision=PRECISE)
        inner_out = inner_out - jnp.einsum("hts,shj->thj", scores, residue, precision=PRECISE)
        inner_state = inner_state - jnp.einsum(
            "shi,sh,shj->hij", key_rows, step_rate, residue, precision=PRECISE
        )
        return (inner_state, inner_out)

    zero_state = jnp.zeros((head_count, HEAD_DIM, HEAD_DIM), jnp.float32)
    _, block_outs = lax.scan(
        jax.checkpoint(advance), zero_state, (split_rows, step_rates, reset_flags)
    )
    inner_out = block_outs.reshape(row_count, head_count, HEAD_DIM)
    centered = inner_out - jnp.mean(inner_out, axis=2, keepdims=True)
    normed = centered * lax.rsqrt(jnp.mean(centered * centered, axis=2, keepdims=True) + 1e-06)
    normed = normed.reshape(row_count, feature_width) * gains + biases
    return normed * jax.nn.gelu(gate_pre)


def on_device(
    tokens,
    out_grad,
    seq_lengths,
    norm_gain,
    in_weight,
    rate_weight,
    init_state,
    mix_gain,
    mix_bias,
    out_weight,
    mlp_gain,
    gate_up,
    down_weight,
):
    row_total = tokens.shape[1]
    model_width = tokens.shape[2]
    group_rows = row_total * lax.axis_size("head")
    local_width = in_weight.shape[2]
    hidden_units = gate_up.shape[2]
    first_gain = norm_gain.astype(jnp.float32)
    second_gain = mlp_gain.astype(jnp.float32)
    source = tokens[0].astype(jnp.float32)
    first_scale = rms_scale(source)
    normed = (source * first_scale * first_gain).astype(jnp.bfloat16)
    gathered = lax.all_gather(normed, "head", axis=0, tiled=True)
    in_flat = in_weight.reshape(model_width, 4 * local_width)
    projected = jnp.dot(gathered, in_flat, preferred_element_type=jnp.float32).reshape(
        group_rows, 4, local_width
    )
    rate_logit = jnp.dot(gathered, rate_weight, preferred_element_type=jnp.float32)
    triple = projected[:, :3].astype(jnp.bfloat16).astype(jnp.float32)
    reset = resets_of(seq_lengths[0], group_rows // MINIBATCH)
    mixed_pre, mixer_back = jax.vjp(
        partial(mixer, reset_flags=reset),
        triple,
        projected[:, 3],
        rate_logit,
        init_state.astype(jnp.float32),
        mix_gain.astype(jnp.float32),
        mix_bias.astype(jnp.float32),
    )
    mixed = mixed_pre.astype(jnp.bfloat16)
    mixed_part = mixed
    branch = lax.psum_scatter(
        jnp.dot(mixed_part, out_weight, preferred_element_type=jnp.float32).astype(jnp.bfloat16),
        "head",
        scatter_dimension=0,
        tiled=True,
    ).astype(jnp.float32)
    hidden = source + branch
    second_scale = rms_scale(hidden)
    normed2 = (hidden * second_scale * second_gain).astype(jnp.bfloat16)
    mlp_in = lax.all_gather(normed2, "mlp", axis=0, tiled=True)
    gate_up_flat = gate_up.reshape(model_width, 2 * hidden_units)
    gate_up_pre = jnp.dot(mlp_in, gate_up_flat, preferred_element_type=jnp.float32).reshape(
        -1, 2, hidden_units
    )
    gate_vals = gate_up_pre[:, 0]
    up_vals = gate_up_pre[:, 1]
    sigmoid_gate = jax.nn.sigmoid(gate_vals)
    silu_gate = gate_vals * sigmoid_gate
    activation = (silu_gate * up_vals).astype(jnp.bfloat16)
    mlp_out = lax.psum_scatter(
        jnp.dot(activation, down_weight, preferred_element_type=jnp.float32).astype(jnp.bfloat16),
        "mlp",
        scatter_dimension=0,
        tiled=True,
    ).astype(jnp.float32)
    result = (hidden + mlp_out).astype(jnp.bfloat16)[None]
    cotangent = out_grad[0]
    cotangent_rows = lax.all_gather(cotangent, "mlp", axis=0, tiled=True)
    grad_down = contract_rows(activation, cotangent_rows)
    d_act = contract_cols(cotangent_rows, down_weight)
    d_gate = d_act * up_vals * (sigmoid_gate + silu_gate * (1.0 - sigmoid_gate))
    d_up = d_act * silu_gate
    d_gate_up = jnp.stack([d_gate, d_up], axis=1).astype(jnp.bfloat16).reshape(-1, 2 * hidden_units)
    grad_gate_up = contract_rows(mlp_in, d_gate_up).reshape(model_width, 2, hidden_units)
    grad_part = d_gate_up
    d_normed2 = lax.psum_scatter(
        contract_cols(grad_part, gate_up_flat).astype(jnp.bfloat16),
        "mlp",
        scatter_dimension=0,
        tiled=True,
    ).astype(jnp.float32)
    grad_mlp_gain = jnp.sum(d_normed2 * hidden * second_scale, axis=0)
    d_hidden = cotangent.astype(jnp.float32) + norm_back(
        hidden, second_scale, second_gain, d_normed2
    )
    d_branch = d_hidden.astype(jnp.bfloat16)
    shard_rows = lax.all_gather(d_branch, "head", axis=0, tiled=True)
    mixed_part = mixed
    weight_sum = contract_rows(mixed_part, shard_rows)
    rows_back = contract_cols(shard_rows, out_weight).astype(jnp.bfloat16)
    grad_out_weight = weight_sum
    d_triple, d_gate_pre, d_rate_logit, grad_init_state, grad_mix_gain, grad_mix_bias = mixer_back(
        rows_back.astype(jnp.float32)
    )
    d_projected = (
        jnp.concatenate([d_triple, d_gate_pre[:, None]], axis=1)
        .astype(jnp.bfloat16)
        .reshape(group_rows, 4 * local_width)
    )
    d_rate = d_rate_logit.astype(jnp.bfloat16)
    grad_in_weight = contract_rows(gathered, d_projected).reshape(model_width, 4, local_width)
    grad_rate_weight = contract_rows(gathered, d_rate)
    grad_part = d_projected
    d_normed = lax.psum_scatter(
        (contract_cols(grad_part, in_flat) + contract_cols(d_rate, rate_weight)).astype(
            jnp.bfloat16
        ),
        "head",
        scatter_dimension=0,
        tiled=True,
    ).astype(jnp.float32)
    grad_norm_gain = jnp.sum(d_normed * source * first_scale, axis=0)
    grad_tokens = d_hidden + norm_back(source, first_scale, first_gain, d_normed)
    (
        grad_in_weight,
        grad_rate_weight,
        grad_init_state,
        grad_mix_gain,
        grad_mix_bias,
        grad_out_weight,
        grad_norm_gain,
        grad_mlp_gain,
    ) = (
        lax.psum(grad_in_weight.astype(jnp.bfloat16), "mlp").astype(jnp.float32),
        lax.psum(grad_rate_weight.astype(jnp.bfloat16), "mlp").astype(jnp.float32),
        lax.psum(grad_init_state.astype(jnp.bfloat16), "mlp").astype(jnp.float32),
        lax.psum(grad_mix_gain.astype(jnp.bfloat16), "mlp").astype(jnp.float32),
        lax.psum(grad_mix_bias.astype(jnp.bfloat16), "mlp").astype(jnp.float32),
        lax.psum(grad_out_weight.astype(jnp.bfloat16), "mlp").astype(jnp.float32),
        lax.psum(grad_norm_gain.astype(jnp.bfloat16), "mlp").astype(jnp.float32),
        lax.psum(grad_mlp_gain.astype(jnp.bfloat16), "mlp").astype(jnp.float32),
    )
    grad_gate_up, grad_down, grad_norm_gain, grad_mlp_gain = (
        lax.psum(grad_gate_up.astype(jnp.bfloat16), "head").astype(jnp.float32),
        lax.psum(grad_down.astype(jnp.bfloat16), "head").astype(jnp.float32),
        lax.psum(grad_norm_gain.astype(jnp.bfloat16), "head").astype(jnp.float32),
        lax.psum(grad_mlp_gain.astype(jnp.bfloat16), "head").astype(jnp.float32),
    )
    return (
        result,
        grad_tokens[None],
        grad_norm_gain,
        grad_in_weight,
        grad_rate_weight,
        grad_init_state,
        grad_mix_gain,
        grad_mix_bias,
        grad_out_weight,
        grad_mlp_gain,
        grad_gate_up,
        grad_down,
    )


def solution(mesh):
    return jax.shard_map(
        on_device,
        mesh=mesh,
        in_specs=(
            P("mlp", "head", None),
            P("mlp", "head", None),
            P("mlp", None),
            P(),
            P(None, None, "head"),
            P(None, "head"),
            P("head", None, None),
            P("head"),
            P("head"),
            P("head", None),
            P(),
            P(None, None, "mlp"),
            P("mlp", None),
        ),
        out_specs=(
            P("mlp", "head", None),
            P("mlp", "head", None),
            P(),
            P(None, None, "head"),
            P(None, "head"),
            P("head", None, None),
            P("head"),
            P("head"),
            P("head", None),
            P(),
            P(None, None, "mlp"),
            P("mlp", None),
        ),
        check_vma=False,
    )
```

profile of v0, /device:TPU:0, one launch (start us, length us, event | category | flops | bytes accessed | tf_op | source)
XLA Modules:
  0.0 1631.4 jit_solution(1207023439945208362)
XLA Ops:
  23.2 6.6 copy.137
  29.8 32.6 %all-gather.6.cloned.1.call-done = bf16[1024,2048]{1,0:T(8,128)(2,1)} async-done(((bf16[128,2048]{1,0:T(8,128)(2,1)}), bf16[1024,2048]{1,0:T(8,128)(2,1)}) %all-gather.6.cloned.1.call-update) | async-done | bytes 4194320 | tf_op jit(solution)/shard_map/all_gather | solution.py:109
  67.3 7.6 fusion.59
  88.9 6.4 copy.139
  95.3 349.7 %while.36 = (s32[]{:T(128)}, f32[4,64,64]{2,1,0:T(8,128)S(1)}, f32[64,16,4,64]{3,1,2,0:T(8,128)S(1)}, f32[64,4,64,64]{3,2,1,0:T(8,128)}, f32[64]{0:T(128)S(1)}, ...) while((s32[]{:T(128)}, f32[4,64,64]{2,1,0:T(8,128)S(1)}, ...), condition=%wide.region_4.5_spmd.clone, body=%wide.region_3.4_spmd.clone.sunk | while | flops 11123204 | bytes 1361840 | solution.py:74
  467.6 48.2 %reduce-scatter.5.cloned.1.call-done = bf16[128,2048]{1,0:T(8,128)(2,1)} async-done(((bf16[1024,2048]{1,0:T(8,128)(2,1)}), bf16[128,2048]{1,0:T(8,128)(2,1)}) %reduce-scatter.5.cloned.1.call-update) | async-done | bytes 524304 | tf_op jit(solution)/shard_map/reduce_scatter | solution.py:128
  520.1 33.0 %all-gather.8.cloned.1.call-done = bf16[512,2048]{1,0:T(8,128)(2,1)} async-done(((bf16[128,2048]{1,0:T(8,128)(2,1)}), bf16[512,2048]{1,0:T(8,128)(2,1)}) %all-gather.8.cloned.1.call-update) | async-done | bytes 2097168 | tf_op jit(solution)/shard_map/all_gather | solution.py:137
  553.1 12.4 fusion.54
  565.5 24.7 %all-gather.12.cloned.1.call-done = bf16[1,512,2048]{2,1,0:T(8,128)(2,1)} async-done(((bf16[1,128,2048]{2,1,0:T(8,128)(2,1)}), bf16[1,512,2048]{2,1,0:T(8,128)(2,1)}) %all-gather.12.cloned.1.call-update) | async-done | bytes 2097168 | tf_op jit(solution)/shard_map/all_gather | solution.py:155
  590.2 8.9 multiply_bitcast_fusion.1
  600.7 10.0 bitcast_convert_fusion
  610.7 35.3 %reduce-scatter.9.cloned.1.call-done = bf16[128,2048]{1,0:T(8,128)(2,1)} async-done(((bf16[512,2048]{1,0:T(8,128)(2,1)}), bf16[128,2048]{1,0:T(8,128)(2,1)}) %reduce-scatter.9.cloned.1.call-update) | async-done | bytes 524304 | tf_op jit(solution)/shard_map/reduce_scatter | solution.py:163
  662.9 8.7 convolution_convert_fusion
  671.7 26.7 %all-gather.10.cloned.1.call-done = bf16[1024,2048]{1,0:T(8,128)(2,1)} async-done(((bf16[128,2048]{1,0:T(8,128)(2,1)}), bf16[1024,2048]{1,0:T(8,128)(2,1)}) %all-gather.10.cloned.1.call-update) | async-done | bytes 4194320 | tf_op jit(solution)/shard_map/all_gather | solution.py:174
  727.9 8.2 fusion.67
  739.4 646.9 %while.37 = (s32[]{:T(128)}, f32[4,64,64]{2,1,0:T(8,128)S(1)}, f32[4,64,64]{2,1,0:T(8,128)S(1)}, bf16[64,16,3,4,64]{4,3,1,0,2:T(4,128)(2,1)}, f32[64,16,4]{1,2,0...) while((s32[]{:T(128)}, f32[4,64,64]{2,1,0:T(8,128)S(1)}, ...), condition=%wide.region_16.17_spmd.clone, body=%wide.region_14.16_spmd.clone.sunk | while | flops 26259908 | bytes 2755820 | solution.py:74
  1403.7 6.5 fusion.62
  1421.7 7.3 convolution_convert_fusion.3
  1429.0 13.9 convert_element_type.219
  1449.6 80.8 %all-reduce.12.cloned.1.call-done = (bf16[2048,4,256]{2,0,1:T(8,128)(2,1)}, bf16[256,2048]{1,0:T(8,128)(2,1)}) async-done(((bf16[2048,4,256]{2,0,1:T(8,128)(2,1)}, bf16[256,2048]{1,0:T(8,128)(2,1)}), (bf16[2048,4,256]{2,0,1:T(8,128)(2,1)}, bf16[256,2048]{1,0:T(8,128)(2,1)})) %all-reduce.12.cloned.1.call-update) | async-done | bytes 5242896 | tf_op jit(solution)/shard_map/psum | solution.py:211
  1533.3 8.5 copy.168
  1541.7 41.1 %reduce-scatter.11.cloned.1.call-done = bf16[128,2048]{1,0:T(8,128)(2,1)} async-done(((bf16[1024,2048]{1,0:T(8,128)(2,1)}), bf16[128,2048]{1,0:T(8,128)(2,1)}) %reduce-scatter.11.cloned.1.call-update) | async-done | bytes 524304 | tf_op jit(solution)/shard_map/reduce_scatter | solution.py:191
  1584.3 19.0 %all-reduce.5 = (bf16[2048]{0:T(1024)(128)(2,1)S(1)}, bf16[2048]{0:T(1024)(128)(2,1)S(1)}, bf16[2048,4]{0,1:T(4,128)(2,1)S(1)}, bf16[4,64,64]{2,1,0:T(8,128)(2,1...) all-reduce(bf16[2048]{0:T(1024)(128)(2,1)S(1)} %get-tuple-element.5, ...), channel_id=1, replica_groups=mesh['head'=8,'mlp'=4] {'mlp'}, use_global_device_ids=true, to_apply=%region_20.21 | all-reduce | flops 29184 | bytes 116736 | tf_op jit(solution)/shard_map/psum | solution.py:217
  1604.5 13.9 all-reduce.3
  (2544 shorter events, 1062.8 us)
Async XLA Ops:
  7.2 456.4 %copy-start = (bf16[256,2048]{1,0:T(8,128)(2,1)S(1)}, bf16[256,2048]{1,0:T(8,128)(2,1)}, u32[]{:S(2)}) copy-start(bf16[256,2048]{1,0:T(8,128)(2,1)} %param.26) | copy-start | bytes 3145732
  7.2 55.2 %all-gather.6.cloned.1.call-start = ((), (), s32[]{:S(2)}) async-start(), calls=%async_computation.4 | async-start | bytes 4718592 | tf_op jit(solution)/shard_map/all_gather | solution.py:109
  12.4 503.4 %reduce-scatter.5.cloned.1.call-start = ((), (), s32[]{:S(2)}) async-start(), calls=%async_computation.5 | async-start | bytes 4718592 | tf_op jit(solution)/shard_map/reduce_scatter | solution.py:128
  466.9 86.2 %all-gather.8.cloned.1.call-start = ((), (), s32[]{:S(2)}) async-start(), calls=%async_computation.6 | async-start | bytes 2621440 | tf_op jit(solution)/shard_map/all_gather | solution.py:137
  467.6 180.7 %copy-start.29 = (f32[2048]{0:T(1024)}, f32[2048]{0:T(1024)S(1)}, u32[]{:S(2)}) copy-start(f32[2048]{0:T(1024)S(1)} %convert_element_type.182) | copy-start | bytes 24580
  517.3 131.1 %copy-start.42 = (f32[128]{0:T(128)}, f32[128]{0:T(128)S(1)}, u32[]{:S(2)}) copy-start(f32[128]{0:T(128)S(1)} %get-tuple-element.617) | copy-start | bytes 1540
  517.3 131.1 %copy-start.51 = (f32[128]{0:T(128)}, f32[128]{0:T(128)S(1)}, u32[]{:S(2)}) copy-start(f32[128]{0:T(128)S(1)} %get-tuple-element.616) | copy-start | bytes 1540
  519.5 70.7 %all-gather.12.cloned.1.call-start = ((), (), s32[]{:S(2)}) async-start(), calls=%async_computation.11 | async-start | bytes 2621440 | tf_op jit(solution)/shard_map/all_gather | solution.py:155
  520.1 125.9 %reduce-scatter.9.cloned.1.call-start = ((), (), s32[]{:S(2)}) async-start(), calls=%async_computation.8 | async-start | bytes 2621440 | tf_op jit(solution)/shard_map/reduce_scatter | solution.py:163
  610.7 87.8 %all-gather.10.cloned.1.call-start = ((), (), s32[]{:S(2)}) async-start(), calls=%async_computation.9 | async-start | bytes 4718592 | tf_op jit(solution)/shard_map/all_gather | solution.py:174
  651.1 777.9 %all-reduce.10.cloned.1.call-start = ((), (), s32[]{:S(2)}) async-start(), calls=%async_computation.12 | async-start | bytes 33816576 | tf_op jit(solution)/shard_map/psum | solution.py:221
  671.7 858.7 %all-reduce.12.cloned.1.call-start = ((), (), s32[]{:S(2)}) async-start(), calls=%async_computation.13 | async-start | bytes 10485760 | tf_op jit(solution)/shard_map/psum | solution.py:211
  739.4 647.5 %copy-start.5 = (f32[1024,256]{0,1:T(8,128)S(1)}, f32[1024,256]{0,1:T(8,128)}, u32[]{:S(2)}) copy-start(f32[1024,256]{0,1:T(8,128)} %copy.145) | copy-start | bytes 3145732
  739.4 647.6 %copy-start.19 = (bf16[1024,256]{0,1:T(8,128)(2,1)S(1)}, bf16[1024,256]{0,1:T(8,128)(2,1)}, u32[]{:S(2)}) copy-start(bf16[1024,256]{0,1:T(8,128)(2,1)} %get-tuple-element.620) | copy-start | bytes 1572868
  739.4 647.6 %copy-start.26 = (f32[1024,4]{0,1:T(4,128)S(1)}, f32[1024,4]{0,1:T(4,128)}, u32[]{:S(2)}) copy-start(f32[1024,4]{0,1:T(4,128)} %copy-done.25) | copy-start | bytes 49156
  739.4 647.5 %copy-start.41 = (f32[256]{0:T(256)S(1)}, f32[256]{0:T(256)}, u32[]{:S(2)}) copy-start(f32[256]{0:T(256)} %convert_element_type.177) | copy-start | bytes 3076
  739.4 647.5 %copy-start.47 = (f32[256]{0:T(256)S(1)}, f32[256]{0:T(256)}, u32[]{:S(2)}) copy-start(f32[256]{0:T(256)} %convert_element_type.178) | copy-start | bytes 3076
  1410.2 172.6 %reduce-scatter.11.cloned.1.call-start = ((), (), s32[]{:S(2)}) async-start(), calls=%async_computation.10 | async-start | bytes 4718592 | tf_op jit(solution)/shard_map/reduce_scatter | solution.py:191
  1420.3 200.6 %reduce-scatter.7.cloned.1.call-start = ((), (), s32[]{:S(2)}) async-start(), calls=%async_computation.7 | async-start | bytes 2621440 | tf_op jit(solution)/shard_map/reduce_scatter | solution.py:147
  1533.2 87.7 %copy-start.6 = (bf16[128,2048]{1,0:T(8,128)(2,1)S(1)}, bf16[128,2048]{1,0:T(8,128)(2,1)}, u32[]{:S(2)}) copy-start(bf16[128,2048]{1,0:T(8,128)(2,1)} %reduce-scatter.5.cloned.1.call-done) | copy-start | bytes 1572868
  1533.2 87.7 %copy-start.12 = (bf16[1,128,2048]{2,1,0:T(8,128)(2,1)S(1)}, bf16[1,128,2048]{2,1,0:T(8,128)(2,1)}, u32[]{:S(2)}) copy-start(bf16[1,128,2048]{2,1,0:T(8,128)(2,1)} %param.18) | copy-start | bytes 1572868
  1533.2 87.7 %copy-start.13 = (bf16[128,2048]{1,0:T(8,128)(2,1)S(1)}, bf16[128,2048]{1,0:T(8,128)(2,1)}, u32[]{:S(2)}) copy-start(bf16[128,2048]{1,0:T(8,128)(2,1)} %reduce-scatter.9.cloned.1.call-done) | copy-start | bytes 1572868
  1533.2 87.7 %copy-start.30 = (f32[2048]{0:T(1024)S(1)}, f32[2048]{0:T(1024)}, u32[]{:S(2)}) copy-start(f32[2048]{0:T(1024)} %copy-done.29) | copy-start | bytes 24580
  1533.2 87.7 %copy-start.43 = (f32[128]{0:T(128)S(1)}, f32[128]{0:T(128)}, u32[]{:S(2)}) copy-start(f32[128]{0:T(128)} %copy-done.42) | copy-start | bytes 1540
  (50 other events, 790.2 us)
Sparse Core Ops, SparseCore 0:
  12.5 49.8 all-gather.5
  467.1 48.7 reduce-scatter.4
  519.6 33.4 all-gather.7
  554.8 35.2 all-gather.11
  610.8 35.1 reduce-scatter.8
  651.3 47.1 all-gather.9
  701.8 334.7 all-reduce.9
  1410.3 119.9 all-reduce.11
  1532.8 49.9 reduce-scatter.10
  1585.9 34.3 reduce-scatter.6
where the time goes:
time: 1660 us; the launch traced here: 1630 us
  local copies, waits for them, and re-layouts  512 us (31%)
  matrix products  431 us (26%)
  waiting for transfers between devices  323 us (19%)
  other arithmetic  223 us (13%)
  loops' own time  93.2 us (6%)
  blocking collectives  32.9 us (2%)
    squeeze x256, local copies, waits for them, and re-layouts, mixer(): lax.scan(jax.checkpoint(advance), zero_state, (split_rows, step_rates, re...  218 us
    dot_general x256, matrix products, advance(): jnp.einsum('thi,hij->thj', key_rows, inner_state, precision=PRECISE)  125 us
    dynamic_slice x256, local copies, waits for them, and re-layouts, mixer(): lax.scan(jax.checkpoint(advance), zero_state, (split_rows, step_rates, re...  124 us
    another operation x2, loops' own time, mixer(): lax.scan(jax.checkpoint(advance), zero_state, (split_rows, step_rates, re...  93.2 us
    add x128, other arithmetic, advance(): inner_state = reset_flag * initial + (1.0 - reset_flag) * inner_state  85.2 us
    psum x1, waiting for transfers between devices, on_device(): lax.psum(grad_in_weight.astype(jnp.bfloat16), 'mlp').astype(jnp.float32)  80.8 us
    dot_general x192, matrix products, advance(): jnp.einsum('shi,sh,shj->hij', key_rows, step_rate, residue, precision=PRE...  65.7 us
    dot_general x192, matrix products, advance(): jnp.einsum('thi,hij->thj', queries, inner_state, precision=PRECISE)  59.8 us
  transfers between devices with their start and end apart: 10, of which 8 were waited for; matrix products, arithmetic and copies ran while one was open for 47% of the time, Pallas kernels for 0%

commit v1 on v0

v1 whole, which is shorter than its diff:
```python
import jax
import jax.numpy as jnp
from jax import lax
from jax.experimental import pallas as pl
from jax.experimental.pallas import tpu as pltpu
from jax.sharding import PartitionSpec as P

HEAD_DIM = 64
MINIBATCH = 16
CHUNK = 128
LANES = 128
VMEM_MOST = 62 * 1024 * 1024
PAIR = LANES // HEAD_DIM
F32 = jnp.float32
BF16 = jnp.bfloat16


def mm(left, right):
    return jnp.dot(left.astype(BF16), right.astype(BF16), preferred_element_type=F32)


def mm_nt(left, right):
    return lax.dot_general(
        left.astype(BF16), right.astype(BF16), (((1,), (1,)), ((), ())), preferred_element_type=F32
    )


def mm_tn(left, right):
    return lax.dot_general(
        left.astype(BF16), right.astype(BF16), (((0,), (0,)), ((), ())), preferred_element_type=F32
    )


def mm_split(left, right):
    high = left.astype(BF16)
    rest = (left - high.astype(F32)).astype(BF16)
    return mm(high, right) + mm(rest, right)


def chunk_masks(len_ref, chunk):
    steps = CHUNK // MINIBATCH
    base = chunk * steps
    row = lax.broadcasted_iota(jnp.int32, (CHUNK, CHUNK), 0)
    col = lax.broadcasted_iota(jnp.int32, (CHUNK, CHUNK), 1)
    row_step = row // MINIBATCH
    col_step = col // MINIBATCH
    row_seq = jnp.zeros((CHUNK, CHUNK), jnp.int32)
    col_seq = jnp.zeros((CHUNK, CHUNK), jnp.int32)
    before = jnp.int32(0)
    last = jnp.int32(0)
    start = jnp.int32(0)
    for at in range(len_ref.shape[1]):
        edge = start - base
        row_seq += (row_step >= edge).astype(jnp.int32)
        col_seq += (col_step >= edge).astype(jnp.int32)
        before += (edge <= -1).astype(jnp.int32)
        last += (edge <= steps - 1).astype(jnp.int32)
        start = start + len_ref[0, at]
    same = row_seq == col_seq
    earlier = jnp.where(same & (col_step < row_step), 1.0, 0.0).astype(F32)
    causal = jnp.where(same & (col <= row), 1.0, 0.0).astype(F32)
    carried = jnp.where(row_seq == before, 1.0, 0.0).astype(F32)
    final = jnp.where(row_seq == last, 1.0, 0.0).astype(F32)
    keep = jnp.where(before == last, 1.0, 0.0).astype(F32)
    return earlier, causal, carried, final, keep


def half_masks():
    lane = lax.broadcasted_iota(jnp.int32, (CHUNK, LANES), 1)
    return [jnp.where(lane // HEAD_DIM == at, 1.0, 0.0).astype(BF16) for at in range(PAIR)]


def same_head(dtype):
    row = lax.broadcasted_iota(jnp.int32, (LANES, LANES), 0) // HEAD_DIM
    col = lax.broadcasted_iota(jnp.int32, (LANES, LANES), 1) // HEAD_DIM
    return jnp.where(row == col, 1.0, 0.0).astype(dtype)


def spread_pair(first, second):
    zero = jnp.zeros((HEAD_DIM, HEAD_DIM), F32)
    return jnp.concatenate(
        [
            jnp.concatenate([first, zero], axis=1),
            jnp.concatenate([zero, second], axis=1),
        ],
        axis=0,
    )


def rates_of(proj_ref, width):
    return jax.nn.sigmoid(proj_ref[:, 4 * width : 4 * width + LANES])


def spread_rate(rates, pair):
    lane = lax.broadcasted_iota(jnp.int32, (CHUNK, LANES), 1)
    first = rates[:, PAIR * pair : PAIR * pair + 1]
    second = rates[:, PAIR * pair + 1 : PAIR * pair + 2]
    return jnp.where(lane < HEAD_DIM, first, second) * (1.0 / (MINIBATCH * HEAD_DIM))


GELU_A = 0.7978845608028654
GELU_B = 0.044715


def gelu_parts(x):
    square = x * x
    bend = jnp.tanh(GELU_A * x * (1.0 + GELU_B * square))
    half = 0.5 * (1.0 + bend)
    slope = half + 0.5 * x * (1.0 - bend * bend) * GELU_A * (1.0 + 3.0 * GELU_B * square)
    return x * half, slope


def scaled_parts(proj_ref, pair, width, rates):
    def part(at):
        return proj_ref[:, at * width + pair * LANES : at * width + (pair + 1) * LANES]

    query = part(0).astype(BF16)
    key = part(1).astype(BF16)
    scaled_key = (key.astype(F32) * spread_rate(rates, pair)).astype(BF16)
    return query, key, scaled_key, part


def forward_local(len_ref, proj_ref, t_ref, a_ref, chunk):
    heads = t_ref.shape[1]
    width = heads * HEAD_DIM
    earlier, causal, _, _, _ = chunk_masks(len_ref, chunk)
    halves = half_masks()
    rates = rates_of(proj_ref, width)
    for pair in range(heads // PAIR):
        query, key, scaled_key, _ = scaled_parts(proj_ref, pair, width, rates)
        for at in range(PAIR):
            head = PAIR * pair + at
            one = -earlier * mm_nt(key * halves[at], scaled_key)
            a_ref[0, head] = (causal * mm_nt(query * halves[at], scaled_key)).astype(BF16)
            one_low = one.astype(BF16)
            two = mm(one_low, one_low)
            two_low = two.astype(BF16)
            total = one + two + mm(two_low, one_low)
            four = mm(two_low, two_low)
            t_ref[0, head] = (total + four + mm(four, total)).astype(BF16)


def forward_state(len_ref, proj_ref, init_ref, e_ref, z_ref, s_ref, t_ref, a_ref, state, first, chunk):
    pairs = state.shape[0]
    width = pairs * LANES

    @pl.when(chunk == 0)
    def _():
        for pair in range(pairs):
            spread = spread_pair(
                init_ref[PAIR * pair].astype(F32), init_ref[PAIR * pair + 1].astype(F32)
            )
            first[pair] = spread
            state[pair] = spread

    _, _, carried, final, keep = chunk_masks(len_ref, chunk)
    halves = half_masks()
    block = same_head(F32)
    rates = rates_of(proj_ref, width)
    outs = []
    for pair in range(pairs):
        lanes = slice(pair * LANES, (pair + 1) * LANES)
        query, key, scaled_key, part = scaled_parts(proj_ref, pair, width, rates)
        value = part(2).astype(BF16).astype(F32)
        now = state[pair]
        start = first[pair]
        both = jnp.concatenate([now, start], axis=1).astype(BF16)
        s_ref[0, pair] = now.astype(BF16)
        key_state = mm(key, both)
        query_state = mm(query, both)
        target = jnp.where(carried > 0.5, key_state[:, :LANES], key_state[:, LANES:]) - value
        target_low = target.astype(BF16)
        error = target
        for at in range(PAIR):
            error = error + mm(t_ref[0, PAIR * pair + at], target_low * halves[at])
        error_low = error.astype(BF16)
        e_ref[:, lanes] = error_low
        state[pair] = (
            keep * now + (1.0 - keep) * start - block * mm_tn(scaled_key * final.astype(BF16), error_low)
        )
        out = jnp.where(carried > 0.5, query_state[:, :LANES], query_state[:, LANES:])
        for at in range(PAIR):
            out = out - mm(a_ref[0, PAIR * pair + at], error_low * halves[at])
        z_ref[:, lanes] = out
        outs.append(out)
    return outs


def forward_tail(outs, gates, gain_ref, bias_ref, mixed_ref):
    mean = same_head(BF16) * (1.0 / HEAD_DIM)
    for pair, out in enumerate(outs):
        lanes = slice(pair * LANES, (pair + 1) * LANES)
        centered = out - mm_split(out, mean)
        normed = centered * lax.rsqrt(mm_split(centered * centered, mean) + 1e-06)
        gelu, _ = gelu_parts(gates[:, lanes])
        mixed_ref[:, lanes] = ((normed * gain_ref[:, lanes] + bias_ref[:, lanes]) * gelu).astype(BF16)


def forward_kernel(len_ref, proj_ref, init_ref, gain_ref, bias_ref, mixed_ref, e_ref, z_ref, s_ref, t_ref, a_ref, state, first):
    chunk = pl.program_id(0)
    width = mixed_ref.shape[1]
    forward_local(len_ref, proj_ref, t_ref, a_ref, chunk)
    outs = forward_state(
        len_ref, proj_ref, init_ref, e_ref, z_ref, s_ref, t_ref, a_ref, state, first, chunk
    )
    forward_tail(outs, proj_ref[:, 3 * width : 4 * width], gain_ref, bias_ref, mixed_ref)


def backward_kernel(
    len_ref, dm_ref, proj_ref, init_ref, gain_ref, bias_ref, e_ref, z_ref, s_ref, t_ref, a_ref,
    dproj_ref, dinit_ref, dgain_ref, dbias_ref, grad, first, dfirst,
):
    step = pl.program_id(0)
    chunks = pl.num_programs(0)
    chunk = chunks - 1 - step
    pairs = grad.shape[0]
    width = pairs * LANES

    @pl.when(step == 0)
    def _():
        for pair in range(pairs):
            first[pair] = spread_pair(
                init_ref[PAIR * pair].astype(F32), init_ref[PAIR * pair + 1].astype(F32)
            ).astype(BF16)
        grad[...] = jnp.zeros_like(grad)
        dfirst[...] = jnp.zeros_like(dfirst)
        dgain_ref[...] = jnp.zeros_like(dgain_ref)
        dbias_ref[...] = jnp.zeros_like(dbias_ref)

    earlier, causal, carried, final, keep = chunk_masks(len_ref, chunk)
    halves = half_masks()
    block = same_head(F32)
    mean = same_head(BF16) * (1.0 / HEAD_DIM)
    rates = rates_of(proj_ref, width)
    drate = jnp.zeros((CHUNK, LANES), F32)
    for pair in range(pairs):
        lanes = slice(pair * LANES, (pair + 1) * LANES)

        def spot(at):
            return slice(at * width + pair * LANES, at * width + (pair + 1) * LANES)

        query = proj_ref[:, spot(0)].astype(BF16)
        key = proj_ref[:, spot(1)].astype(BF16)
        gate = proj_ref[:, spot(3)]
        rate = spread_rate(rates, pair)
        key_wide = key.astype(F32)
        scaled_key = (key_wide * rate).astype(BF16)
        out = z_ref[:, lanes]
        centered = out - mm_split(out, mean)
        scale = lax.rsqrt(mm_split(centered * centered, mean) + 1e-06)
        normed = centered * scale
        gain = gain_ref[:, lanes]
        gelu, slope = gelu_parts(gate)
        dmixed = dm_ref[:, lanes].astype(F32)
        dy = dmixed * gelu
        dproj_ref[:, spot(3)] = (dmixed * (normed * gain + bias_ref[:, lanes]) * slope).astype(BF16)
        dgain_ref[:, lanes] += jnp.sum(dy * normed, axis=0, keepdims=True)
        dbias_ref[:, lanes] += jnp.sum(dy, axis=0, keepdims=True)
        dnormed = dy * gain
        dout = scale * (dnormed - mm_split(dnormed, mean) - normed * mm_split(dnormed * normed, mean))
        dout_low = dout.astype(BF16)
        error = e_ref[:, lanes]
        upper = grad[pair]
        upper_low = upper.astype(BF16)
        derror = -rate * final * mm(key, upper_low)
        for at in range(PAIR):
            derror = derror - mm_tn(a_ref[0, PAIR * pair + at], dout_low * halves[at])
        derror_low = derror.astype(BF16)
        dtarget = derror
        for at in range(PAIR):
            dtarget = dtarget + mm_tn(t_ref[0, PAIR * pair + at], derror_low * halves[at])
        dtarget_low = dtarget.astype(BF16)
        dproj_ref[:, spot(2)] = (-dtarget).astype(BF16)
        both = jnp.concatenate([s_ref[0, pair], first[pair]], axis=0)
        from_out = mm_nt(dout_low, both)
        from_target = mm_nt(dtarget_low, both)
        dquery = jnp.where(carried > 0.5, from_out[:, :LANES], from_out[:, LANES:])
        dkey = jnp.where(carried > 0.5, from_target[:, :LANES], from_target[:, LANES:])
        dscaled = -final * mm_nt(error, upper_low)
        for at in range(PAIR):
            dscore = (-causal * mm_nt(dout_low * halves[at], error)).astype(BF16)
            dlower = (-earlier * mm_nt(dtarget_low * halves[at], error)).astype(BF16)
            part = scaled_key * halves[at]
            dquery = dquery + mm(dscore, part)
            dkey = dkey + mm(dlower, part)
            dscaled = dscaled + mm_tn(dscore, query * halves[at]) + mm_tn(dlower, key * halves[at])
        dkey = dkey + rate * dscaled
        dproj_ref[:, spot(0)] = dquery.astype(BF16)
        dproj_ref[:, spot(1)] = dkey.astype(BF16)
        row_head = lax.broadcasted_iota(jnp.int32, (LANES, LANES), 0) // HEAD_DIM
        col = lax.broadcasted_iota(jnp.int32, (LANES, LANES), 1)
        pick = jnp.where(col == PAIR * pair + row_head, 1.0, 0.0).astype(BF16)
        drate = drate + mm_split(dscaled * key_wide, pick)
        rows = jnp.concatenate([key, query], axis=0)
        carried_low = carried.astype(BF16)
        carried_both = jnp.concatenate([carried_low, carried_low], axis=0)
        kept = rows * carried_both
        sides = jnp.concatenate([kept, rows - kept], axis=1)
        pulled = mm_tn(sides, jnp.concatenate([dtarget_low, dout_low], axis=0))
        grad[pair] = keep * upper + block * pulled[:LANES]
        dfirst[pair] += (1.0 - keep) * upper + block * pulled[LANES:]
    dproj_ref[:, 4 * width :] = (
        drate * rates * (1.0 - rates) * (1.0 / (MINIBATCH * HEAD_DIM))
    ).astype(BF16)

    @pl.when(step == chunks - 1)
    def _():
        for pair in range(pairs):
            dinit_ref[PAIR * pair] = dfirst[pair, :HEAD_DIM, :HEAD_DIM]
            dinit_ref[PAIR * pair + 1] = dfirst[pair, HEAD_DIM:, HEAD_DIM:]


MESH = pl.DeviceIdType.MESH


def chip_peer(hops):
    me = lax.axis_index("head")
    chips = lax.axis_size("head") // 2
    return {"head": lax.rem(me // 2 + hops, chips) * 2 + lax.rem(me, 2)}


def core_peer():
    me = lax.axis_index("head")
    return {"head": me + 1 - 2 * lax.rem(me, 2)}


def head_peer(ahead):
    return {"head": lax.rem(lax.axis_index("head") + ahead, lax.axis_size("head"))}


def mlp_peer(flip):
    me = lax.axis_index("mlp")
    across, along = lax.rem(me, 2), me // 2
    if flip % 2:
        across = 1 - across
    if flip // 2:
        along = 1 - along
    return {"mlp": 2 * along + across}


def greet(peers):
    barrier = pltpu.get_barrier_semaphore()
    for peer in peers:
        pl.semaphore_signal(barrier, inc=1, device_id=peer, device_id_type=MESH)
    pl.semaphore_wait(barrier, len(peers))


def copies_of(moves, send_sems, recv_sems, base=0):
    made = []
    for at, (source, target, peer) in enumerate(moves, base):
        if peer is None:
            made.append(pltpu.make_async_copy(source, target, send_sems.at[at]))
        else:
            made.append(
                pltpu.make_async_remote_copy(
                    src_ref=source,
                    dst_ref=target,
                    send_sem=send_sems.at[at],
                    recv_sem=recv_sems.at[at],
                    device_id=peer,
                    device_id_type=MESH,
                )
            )
    return made


def launch(moves, send_sems, recv_sems, base=0):
    for copy in copies_of(moves, send_sems, recv_sems, base):
        copy.start()


def settle(moves, send_sems, recv_sems, base=0):
    for copy in copies_of(moves, send_sems, recv_sems, base):
        copy.wait()


def anywhere(count):
    return [pl.BlockSpec(memory_space=pl.ANY)] * count


def sem_pair(count):
    return [pltpu.SemaphoreType.DMA((count,)), pltpu.SemaphoreType.DMA((count,))]


def gather_parts(moves, sems):
    copies = [
        pltpu.make_async_copy(source, target, sems.at[at])
        for at, (source, target) in enumerate(moves)
    ]
    for copy in copies:
        copy.start()
    for copy in copies:
        copy.wait()


def near_peers():
    return [mlp_peer(flip) for flip in (1, 2, 3)]


def line_peers():
    return [chip_peer(hops) for hops in (1, 2, 3)]


def line_moves(values, begin, target):
    size = values.shape[0] // 2
    part = values.at[pl.ds(begin * size, size)]
    peers = line_peers()
    return [(part, target.at[pl.ds(at * size, size)], peers[at]) for at in range(3)]


class Carry:
    def __init__(self, arrays=(), out_shape=(), plan=None, count=1, collective_id=None, later=None):
        self.arrays = list(arrays)
        self.out_shape = [jax.ShapeDtypeStruct(shape, BF16) for shape in out_shape]
        self.plan = plan
        self.count = count
        self.collective_id = collective_id
        self.later = later

    def params(self):
        extra = {}
        if self.plan is not None:
            extra = {"collective_id": self.collective_id, "has_side_effects": True}
        return pltpu.CompilerParams(vmem_limit_bytes=VMEM_MOST, **extra)

    def split(self, refs, ins, outs):
        mine, given = len(self.arrays), len(self.out_shape)
        body = refs[:ins] + refs[ins + mine : ins + mine + outs] + refs[ins + mine + outs + given : -2]
        extra_in = refs[ins : ins + mine]
        extra_out = refs[ins + mine + outs : ins + mine + outs + given]
        return body, extra_in, extra_out, refs[-2], refs[-1]

    def wrap(self, body, ins, outs):
        def kernel(*refs):
            own, extra_in, extra_out, send_sems, recv_sems = self.split(refs, ins, outs)
            if self.plan is not None:

                @pl.when(pl.program_id(0) == 0)
                def _():
                    peers, moves = self.plan(extra_in, extra_out)
                    greet(peers)
                    launch(moves, send_sems, recv_sems)

            if self.later is not None:

                @pl.when(pl.program_id(0) == self.later[0])
                def _():
                    moves = self.plan(extra_in, extra_out)[1]
                    settle(moves[: self.later[1]], send_sems, recv_sems)
                    launch(self.later[2](extra_in, extra_out), send_sems, recv_sems, len(moves))

            body(*own)
            if self.plan is not None:

                @pl.when(pl.program_id(0) == pl.num_programs(0) - 1)
                def _():
                    moves = self.plan(extra_in, extra_out)[1]
                    done = 0 if self.later is None else self.later[1]
                    settle(moves[done:], send_sems, recv_sems, done)
                    if self.later is not None:
                        settle(self.later[2](extra_in, extra_out), send_sems, recv_sems, len(moves))

        return kernel


def mixer_forward(lengths, proj, initial, gains, biases, carry):
    rows = proj.shape[0]
    heads = initial.shape[0]
    width = heads * HEAD_DIM
    chunks = rows // CHUNK
    pairs = heads // PAIR
    full = lambda *shape: pl.BlockSpec(shape, lambda c: (0,) * len(shape))
    got = pl.pallas_call(
        carry.wrap(forward_kernel, 5, 6),
        grid=(chunks,),
        in_specs=[
            pl.BlockSpec(memory_space=pltpu.SMEM),
            pl.BlockSpec((CHUNK, proj.shape[1]), lambda c: (c, 0)),
            full(heads, HEAD_DIM, HEAD_DIM),
            full(1, width),
            full(1, width),
            *anywhere(len(carry.arrays)),
        ],
        out_specs=[
            pl.BlockSpec((CHUNK, width), lambda c: (c, 0)),
            pl.BlockSpec((CHUNK, width), lambda c: (c, 0)),
            pl.BlockSpec((CHUNK, width), lambda c: (c, 0)),
            pl.BlockSpec((1, pairs, LANES, LANES), lambda c: (c, 0, 0, 0)),
            pl.BlockSpec((1, heads, CHUNK, CHUNK), lambda c: (c, 0, 0, 0)),
            pl.BlockSpec((1, heads, CHUNK, CHUNK), lambda c: (c, 0, 0, 0)),
            *anywhere(len(carry.out_shape)),
        ],
        out_shape=[
            jax.ShapeDtypeStruct((rows, width), BF16),
            jax.ShapeDtypeStruct((rows, width), BF16),
            jax.ShapeDtypeStruct((rows, width), F32),
            jax.ShapeDtypeStruct((chunks, pairs, LANES, LANES), BF16),
            jax.ShapeDtypeStruct((chunks, heads, CHUNK, CHUNK), BF16),
            jax.ShapeDtypeStruct((chunks, heads, CHUNK, CHUNK), BF16),
            *carry.out_shape,
        ],
        scratch_shapes=[
            pltpu.VMEM((pairs, LANES, LANES), F32),
            pltpu.VMEM((pairs, LANES, LANES), F32),
            *sem_pair(carry.count),
        ],
        compiler_params=carry.params(),
        cost_estimate=pl.CostEstimate(
            flops=rows * width * CHUNK * 40, bytes_accessed=rows * width * 30, transcendentals=rows * width
        ),
        name="mixer_forward",
    )(lengths, proj, initial, gains, biases, *carry.arrays)
    return got[:6], got[6:]


def mixer_backward(lengths, dmixed, proj, initial, gains, biases, kept, carry, places=(0, 0)):
    rows = proj.shape[0]
    heads = initial.shape[0]
    width = heads * HEAD_DIM
    chunks = rows // CHUNK
    pairs = heads // PAIR
    full = lambda *shape: pl.BlockSpec(shape, lambda i: (0,) * len(shape))
    at = lambda *shape: pl.BlockSpec(shape, lambda i: (chunks - 1 - i,) + (0,) * (len(shape) - 1))
    got = pl.pallas_call(
        carry.wrap(backward_kernel, 11, 4),
        grid=(chunks,),
        in_specs=[
            pl.BlockSpec(memory_space=pltpu.SMEM),
            at(CHUNK, width),
            at(CHUNK, proj.shape[1]),
            full(heads, HEAD_DIM, HEAD_DIM),
            pl.BlockSpec((1, width), lambda i: (0, places[0])),
            pl.BlockSpec((1, width), lambda i: (0, places[1])),
            at(CHUNK, width),
            at(CHUNK, width),
            at(1, pairs, LANES, LANES),
            at(1, heads, CHUNK, CHUNK),
            at(1, heads, CHUNK, CHUNK),
            *anywhere(len(carry.arrays)),
        ],
        out_specs=[
            at(CHUNK, proj.shape[1]),
            full(heads, HEAD_DIM, HEAD_DIM),
            full(1, width),
            full(1, width),
            *anywhere(len(carry.out_shape)),
        ],
        out_shape=[
            jax.ShapeDtypeStruct(proj.shape, BF16),
            jax.ShapeDtypeStruct((heads, HEAD_DIM, HEAD_DIM), F32),
            jax.ShapeDtypeStruct((1, width), F32),
            jax.ShapeDtypeStruct((1, width), F32),
            *carry.out_shape,
        ],
        scratch_shapes=[
            pltpu.VMEM((pairs, LANES, LANES), F32),
            pltpu.VMEM((pairs, LANES, LANES), BF16),
            pltpu.VMEM((pairs, LANES, LANES), F32),
            *sem_pair(carry.count),
        ],
        compiler_params=carry.params(),
        cost_estimate=pl.CostEstimate(
            flops=rows * width * CHUNK * 50, bytes_accessed=rows * width * 40, transcendentals=rows * width
        ),
        name="mixer_backward",
    )(lengths, dmixed, proj, initial, gains, biases, *kept, *carry.arrays)
    return got[:4], got[4:]


def head_kernel(*refs):
    len_ref, tokens, rate_rows, init_ref = refs[:4]
    vectors, (weight_raw, cot, out_weight), refs = refs[4:8], refs[8:11], refs[11:]
    proj_ref, rate, mixed_ref, e_ref, z_ref, s_ref, t_ref, a_ref, gain = refs[:9]
    gathered_ref, cot_got, weight_ref, mixed_rows, out_cross, out_other, cot_line, out_line = refs[9:17]
    held, raw, weight, state, first, slots, line_hold, own_hold = refs[17:25]
    line_send, line_recv, core_send, core_recv, near_send, near_recv, out_send, out_recv = refs[25:33]
    keep_sem, weight_sem, row_send, row_recv, cross_send, cross_recv = refs[33:39]
    cot_send, cot_recv, other_send, other_recv, hold_sems = refs[39:]
    me = lax.axis_index("head")
    chip, core = me // 2, lax.rem(me, 2)
    member = lax.axis_index("mlp")
    rows = tokens.shape[0]
    chips = held.shape[0] // (2 * rows)
    sides = [mlp_peer(flip) for flip in (1, 2, 3)]
    others = [chip_peer(hops) for hops in range(1, chips)]
    partner = core_peer()
    load = pltpu.make_async_copy(weight_raw, raw, weight_sem.at[0])
    load.start()
    place_at = 0
    for vector in vectors:
        values = vector[...].astype(F32)
        for at in range(vector.shape[0]):
            gain[:, place_at : place_at + LANES] = values[at : at + 1, :]
            place_at += LANES
    source = tokens[...].astype(F32)
    own_rows = pl.ds(pl.multiple_of(me * rows, rows), rows)
    held[own_rows, :] = (source * rms_scale(source) * gain[:, : source.shape[1]]).astype(BF16)
    rate[...] = jnp.zeros_like(rate)
    rate[: rate_rows.shape[0], :] = rate_rows[...]
    greet([head_peer(ahead) for ahead in range(1, 8)] + sides)

    def place(of_chip, of_core):
        return held.at[pl.ds(pl.multiple_of((of_chip * 2 + of_core) * rows, rows), rows)]

    def hop(of_chip, step):
        side = (step + 1) // 2
        return pltpu.make_async_remote_copy(
            src_ref=place(of_chip, core),
            dst_ref=place(of_chip, core),
            send_sem=line_send.at[side, of_chip],
            recv_sem=line_recv.at[of_chip],
            device_id={"head": me + 2 * step},
            device_id_type=MESH,
        )

    def across(of_chip, of_core):
        return pltpu.make_async_remote_copy(
            src_ref=place(of_chip, of_core),
            dst_ref=place(of_chip, of_core),
            send_sem=core_send.at[of_chip],
            recv_sem=core_recv.at[of_chip],
            device_id=partner,
            device_id_type=MESH,
        )

    quarter = out_weight.shape[0] // 4
    part = out_weight.at[pl.ds(pl.multiple_of(member * quarter, quarter), quarter)]
    near_moves = [(cot, cot_got.at[at], sides[at]) for at in range(3)]
    out_moves = [(part, out_line.at[chip], peer) for peer in others]
    for step in (-1, 1):

        @pl.when(jnp.logical_and(chip + step >= 0, chip + step < chips))
        def _(step=step):
            hop(chip, step).start()

    across(chip, core).start()
    launch(out_moves, out_send, out_recv)
    launch(near_moves, near_send, near_recv)
    def product(of_chip):
        block = pl.ds(pl.multiple_of(of_chip * 2 * rows, 2 * rows), 2 * rows)
        values = held[block, :]
        wide = weight.shape[1]
        proj_ref[block, :wide] = jnp.dot(values, weight[...], preferred_element_type=F32)
        proj_ref[block, wide:] = mm_nt(values, rate[...])
        pltpu.make_async_copy(held.at[block], gathered_ref.at[block], keep_sem.at[of_chip]).start()

    def turn(at):
        if isinstance(at, int) and at == 0:
            return chip
        if isinstance(at, int) and at == 1:
            return chip + 1 - 2 * lax.rem(chip, 2)
        return at - (2 * at - 3) * (chip // 2)

    def arrive(at):
        of_chip = turn(at)
        pltpu.make_async_remote_copy(
            src_ref=place(of_chip, core),
            dst_ref=place(of_chip, core),
            send_sem=line_send.at[0, of_chip],
            recv_sem=line_recv.at[of_chip],
            device_id=partner,
            device_id_type=MESH,
        ).wait_recv()
        for step in (-1, 1):
            wanted = (of_chip > chip) if step < 0 else (of_chip < chip)

            @pl.when(jnp.logical_and(wanted, jnp.logical_and(chip + step >= 0, chip + step < chips)))
            def _(step=step):
                hop(of_chip, step).start()

        across(of_chip, core).start()

    near = sides
    heads = 2 * chips
    ahead = [lax.rem(chip + hops, 4) for hops in (1, 2, 3)]
    local = mixed_ref.shape[1]
    half = quarter // 2
    top, bottom = pl.ds(0, half), pl.ds(half, half)

    def row_copy(sender, target, stays):
        rel = lax.rem(core + target, 2)
        place_at = mixed_rows.at[rel, :, pl.ds(pl.multiple_of(chip * local, local), local)]
        if stays:
            return pltpu.make_async_copy(slots.at[target], place_at, row_send.at[target])
        return pltpu.make_async_remote_copy(
            src_ref=slots.at[target],
            dst_ref=place_at,
            send_sem=row_send.at[target],
            recv_sem=row_recv.at[sender],
            device_id={"head": target},
            device_id_type=MESH,
        )

    def cross_moves(flip):
        if flip < 2:
            return [
                (out_line.at[of_chip], out_cross.at[of_chip, member], near[flip])
                for of_chip in ahead
            ]
        moves = []
        for of_chip in ahead:
            one = out_cross.at[of_chip, near[0]["mlp"], top]
            two = out_cross.at[of_chip, near[1]["mlp"], bottom]
            moves += [(one, one, near[1]), (two, two, near[0])]
        return moves

    def swap_moves(flip):
        of_member = near[flip]["mlp"]
        return [
            (out_cross.at[of_chip, of_member], out_other.at[of_chip, of_member], partner)
            for of_chip in ahead
        ]

    def hold_moves():
        moves = [(line_hold.at[at], out_cross.at[ahead[at], member], None) for at in range(3)]
        moves += [(line_hold.at[at], out_other.at[ahead[at], member], partner) for at in range(3)]
        return moves + [
            (own_hold, out_cross.at[chip], None),
            (own_hold, out_other.at[chip], partner),
        ]

    cot_moves = line_moves(cot, 0, cot_line)
    own_out = [
        pltpu.make_async_copy(
            out_weight.at[pl.ds(at * quarter, quarter)], own_hold.at[at], hold_sems.at[3 + at]
        )
        for at in range(4)
    ]
    for copy in own_out:
        copy.start()

    def local_part(of_chip):
        for of_core in range(2):
            at = of_chip * 2 + of_core
            block = pl.ds(pl.multiple_of(at * CHUNK, CHUNK), CHUNK)
            one = pl.ds(at, 1)
            forward_local(len_ref, proj_ref.at[block], t_ref.at[one], a_ref.at[one], at)

    inner = jnp.logical_and(chip > 0, chip < chips - 1)
    outer = jnp.logical_not(inner)
    arrive(1)
    pl.when(inner)(lambda: arrive(2))
    load.wait()
    wide = raw.shape[2]

    def untie(at, _):
        span = pl.ds(pl.multiple_of(at * 256, 256), 256)
        values = raw[span]
        for part in range(4):
            weight[span, part * wide : (part + 1) * wide] = values[:, part, :]
        return 0

    lax.fori_loop(0, raw.shape[0] // 256, untie, 0)
    store = pltpu.make_async_copy(weight, weight_ref, weight_sem.at[1])
    store.start()

    def gather_step(at, _):
        pl.when(jnp.logical_and(inner, at == 1))(lambda: arrive(3))
        pl.when(jnp.logical_and(outer, at == 2))(lambda: arrive(2))
        pl.when(jnp.logical_and(outer, at == 3))(lambda: arrive(3))

        @pl.when(at == 2)
        def _():
            settle(out_moves, out_send, out_recv)
            for flip in range(2):
                launch(cross_moves(flip), cross_send.at[flip], cross_recv.at[flip])
            gather_parts(
                [(out_line.at[ahead[spot]], line_hold.at[spot]) for spot in range(3)], hold_sems
            )
            for copy in own_out:
                copy.wait()
            launch(hold_moves(), other_send.at[3], other_recv.at[3])

        @pl.when(at == 3)
        def _():
            launch(cot_moves, cot_send, cot_recv)

        of_chip = jnp.where(at == 0, turn(0), jnp.where(at == 1, turn(1), turn(at)))
        across(of_chip, 1 - core).wait_recv()
        product(of_chip)
        local_part(of_chip)
        return 0

    lax.fori_loop(0, chips, gather_step, 0)

    def rows_of(at):
        return pl.ds(pl.multiple_of(at * CHUNK, CHUNK), CHUNK)

    def advance(at):
        block, one = rows_of(at), pl.ds(at, 1)
        return forward_state(
            len_ref,
            proj_ref.at[block],
            init_ref,
            e_ref.at[block],
            z_ref.at[block],
            s_ref.at[one],
            t_ref.at[one],
            a_ref.at[one],
            state,
            first,
            at,
        )

    spot = 2 * tokens.shape[1]
    mix_gain = gain.at[:, pl.ds(spot, local)]
    mix_bias = gain.at[:, pl.ds(spot + local, local)]

    def ship(at):
        mixed_ref[rows_of(at), :] = slots[at]

        @pl.when(at != me)
        def _():
            row_copy(me, at, False).start()

        @pl.when(at == me)
        def _():
            row_copy(me, at, True).start()

    def step(at, outs):
        @pl.when(at == 1)
        def _():
            for flip in range(2):
                settle(cross_moves(flip), cross_send.at[flip], cross_recv.at[flip])
            launch(cross_moves(2), cross_send.at[2], cross_recv.at[2])
            for flip in range(2):
                launch(swap_moves(flip), other_send.at[flip], other_recv.at[flip])

        gates = proj_ref[rows_of(at - 1), 3 * local : 4 * local]
        later = advance(at)
        forward_tail(outs, gates, mix_gain, mix_bias, slots.at[at - 1])
        ship(at - 1)
        return tuple(later)

    outs = lax.fori_loop(1, heads, step, tuple(advance(0)))
    gates = proj_ref[rows_of(heads - 1), 3 * local : 4 * local]
    forward_tail(outs, gates, mix_gain, mix_bias, slots.at[heads - 1])
    ship(heads - 1)
    settle(cross_moves(2), cross_send.at[2], cross_recv.at[2])
    launch(swap_moves(2), other_send.at[2], other_recv.at[2])
    settle(cot_moves, cot_send, cot_recv)
    settle(hold_moves(), other_send.at[3], other_recv.at[3])
    for at in range(8):

        @pl.when(me != at)
        def _(at=at):
            row_copy(me, at, False).wait_send()
            row_copy(at, at, False).wait_recv()

        @pl.when(me == at)
        def _(at=at):
            row_copy(me, at, True).wait()

    for at in range(chips):
        of_chip = turn(at)
        across(of_chip, core).wait_send()
        block = pl.ds(pl.multiple_of(of_chip * 2 * rows, 2 * rows), 2 * rows)
        pltpu.make_async_copy(held.at[block], gathered_ref.at[block], keep_sem.at[of_chip]).wait()
        for step in (-1, 1):
            wanted = (of_chip >= chip) if step < 0 else (of_chip <= chip)

            @pl.when(jnp.logical_and(wanted, jnp.logical_and(chip + step >= 0, chip + step < chips)))
            def _(step=step):
                hop(of_chip, step).wait_send()

    settle(near_moves, near_send, near_recv)
    store.wait()
    for flip in range(3):
        settle(swap_moves(flip), other_send.at[flip], other_recv.at[flip])


def head(lengths, tokens, rate_rows, initial, vectors, in_weight, cot, out_weight, collective_id):
    devices = lax.axis_size("head")
    rows, width = tokens.shape
    heads = initial.shape[0]
    local = heads * HEAD_DIM
    pairs = heads // PAIR
    wide = 4 * in_weight.shape[2]
    chips = devices // 2
    quarters = (4, out_weight.shape[0] // 4, width)
    vmem = pl.BlockSpec(memory_space=pltpu.VMEM)
    got = pl.pallas_call(
        head_kernel,
        in_specs=[pl.BlockSpec(memory_space=pltpu.SMEM)] + [vmem] * 7 + anywhere(3),
        out_specs=[vmem] * 9 + anywhere(8),
        out_shape=[
            jax.ShapeDtypeStruct((devices * rows, wide + LANES), F32),
            jax.ShapeDtypeStruct((LANES, width), BF16),
            jax.ShapeDtypeStruct((devices * rows, local), BF16),
            jax.ShapeDtypeStruct((devices * rows, local), BF16),
            jax.ShapeDtypeStruct((devices * rows, local), F32),
            jax.ShapeDtypeStruct((devices, pairs, LANES, LANES), BF16),
            jax.ShapeDtypeStruct((devices, heads, CHUNK, CHUNK), BF16),
            jax.ShapeDtypeStruct((devices, heads, CHUNK, CHUNK), BF16),
            jax.ShapeDtypeStruct((1, sum(vector.size for vector in vectors)), F32),
            jax.ShapeDtypeStruct((devices * rows, width), BF16),
            jax.ShapeDtypeStruct((3, rows, width), BF16),
            jax.ShapeDtypeStruct((width, wide), BF16),
            jax.ShapeDtypeStruct((2, rows, width // 2), BF16),
            jax.ShapeDtypeStruct((4, *quarters), BF16),
            jax.ShapeDtypeStruct((4, *quarters), BF16),
            jax.ShapeDtypeStruct((3 * rows // 2, width), BF16),
            jax.ShapeDtypeStruct((chips, *quarters[1:]), BF16),
        ],
        scratch_shapes=[
            pltpu.VMEM((devices * rows, width), BF16),
            pltpu.VMEM(in_weight.shape, BF16),
            pltpu.VMEM((width, wide), BF16),
            pltpu.VMEM((pairs, LANES, LANES), F32),
            pltpu.VMEM((pairs, LANES, LANES), F32),
            pltpu.VMEM((devices, CHUNK, local), BF16),
            pltpu.VMEM((3, *quarters[1:]), BF16),
            pltpu.VMEM(quarters, BF16),
            pltpu.SemaphoreType.DMA((2, chips)),
            pltpu.SemaphoreType.DMA((chips,)),
            pltpu.SemaphoreType.DMA((chips,)),
            pltpu.SemaphoreType.DMA((chips,)),
            *sem_pair(3),
            *sem_pair(3),
            pltpu.SemaphoreType.DMA((chips,)),
            pltpu.SemaphoreType.DMA((2,)),
            *sem_pair(8),
            pltpu.SemaphoreType.DMA((3, 6)),
            pltpu.SemaphoreType.DMA((3, 6)),
            *sem_pair(3),
            pltpu.SemaphoreType.DMA((4, 8)),
            pltpu.SemaphoreType.DMA((4, 8)),
            pltpu.SemaphoreType.DMA((7,)),
        ],
        compiler_params=pltpu.CompilerParams(
            vmem_limit_bytes=VMEM_MOST, collective_id=collective_id, has_side_effects=True
        ),
        cost_estimate=pl.CostEstimate(
            flops=2 * devices * rows * width * wide, bytes_accessed=4 * devices * rows * width, transcendentals=0
        ),
        name="head",
    )(lengths, tokens, rate_rows, initial, *vectors, in_weight, cot, out_weight)
    return got[:2], got[2:8], got[8], got[9:16]


UNITS = 704
PLANE_UNITS = 688
SPAN = 512
FINISH = 176


def gated(gate, up):
    sigmoid = jax.nn.sigmoid(gate)
    silu = gate * sigmoid
    return silu, sigmoid + silu * (1.0 - sigmoid)


def tile(*shape):
    return pl.BlockSpec(shape, (lambda i: (0, i, 0)) if len(shape) == 3 else (lambda i: (i, 0)))


def plane_kernel(*refs):
    x_own, x_got, o_own, o_got, gu_ref, down_ref, dx_ref, out_ref = refs[:8]
    act_ref, d_gate_ref, d_up_ref, x_all, o_all, dx_sum, out_sum, turned, sems = refs[8:]
    rows = x_own.shape[0]
    step = pl.program_id(0)
    last = pl.num_programs(0) - 1

    @pl.when(step == 0)
    def _():
        moves = [(x_own, x_all.at[pl.ds(0, rows)]), (o_own, o_all.at[pl.ds(0, rows)])]
        for at in range(3):
            place = pl.ds((at + 1) * rows, rows)
            moves += [(x_got.at[at], x_all.at[place]), (o_got.at[at], o_all.at[place])]
        gather_parts(moves, sems)

    gate = mm_nt(gu_ref[0], x_all[...])
    up = mm_nt(gu_ref[1], x_all[...])
    d_act = mm_nt(down_ref[...], o_all[...])
    silu, slope = gated(gate, up)
    act = (silu * up).astype(BF16)
    d_gate = (d_act * up * slope).astype(BF16)
    d_up = (d_act * silu).astype(BF16)
    act_ref[...] = act
    d_gate_ref[...] = d_gate
    d_up_ref[...] = d_up
    for at, part in enumerate((d_gate, d_up, act)):
        turned[at] = part.T

    def back(at, _):
        span = pl.ds(pl.multiple_of(at * SPAN, SPAN), SPAN)
        dx = mm(turned[0], gu_ref[0, :, span]) + mm(turned[1], gu_ref[1, :, span])
        out = mm(turned[2], down_ref[:, span])

        @pl.when(step == 0)
        def _():
            dx_sum[:, span] = dx
            out_sum[:, span] = out

        @pl.when(step > 0)
        def _():
            dx_sum[:, span] += dx
            out_sum[:, span] += out

        @pl.when(step == last)
        def _():
            for at in range(4):
                place = pl.ds(at * rows, rows)
                dx_ref[at, :, span] = dx_sum[place, span].astype(BF16)
                out_ref[at, :, span] = out_sum[place, span].astype(BF16)

        return 0

    lax.fori_loop(0, x_all.shape[1] // SPAN, back, 0)


def mlp_plane(x_own, x_got, o_own, o_got, gate_up_rows, down_weight, carry):
    rows, width = x_own.shape
    hidden = down_weight.shape[0]
    whole = pl.BlockSpec((4, rows, width), lambda i: (0, 0, 0))
    got = pl.pallas_call(
        carry.wrap(plane_kernel, 6, 5),
        grid=(hidden // PLANE_UNITS,),
        in_specs=anywhere(4)
        + [tile(2, PLANE_UNITS, width), tile(PLANE_UNITS, width)]
        + anywhere(len(carry.arrays)),
        out_specs=[whole, whole]
        + [tile(PLANE_UNITS, 4 * rows)] * 3
        + anywhere(len(carry.out_shape)),
        out_shape=[jax.ShapeDtypeStruct((4, rows, width), BF16)] * 2
        + [jax.ShapeDtypeStruct((hidden, 4 * rows), BF16)] * 3
        + carry.out_shape,
        scratch_shapes=[
            pltpu.VMEM((4 * rows, width), BF16),
            pltpu.VMEM((4 * rows, width), BF16),
            pltpu.VMEM((4 * rows, width), F32),
            pltpu.VMEM((4 * rows, width), F32),
            pltpu.VMEM((3, 4 * rows, PLANE_UNITS), BF16),
            pltpu.SemaphoreType.DMA((8,)),
            *sem_pair(carry.count),
        ],
        compiler_params=carry.params(),
        cost_estimate=pl.CostEstimate(
            flops=48 * rows * hidden * width, bytes_accessed=6 * hidden * width, transcendentals=4 * rows * hidden
        ),
        name="mlp_plane",
    )(x_own, x_got, o_own, o_got, gate_up_rows, down_weight, *carry.arrays)
    return got[:2], got[2:5], got[5:]


def grads_kernel(*refs):
    x_own, x_got, x_far, o_own, o_got, o_far = refs[0], refs[1], refs[2:10], refs[10], refs[11], refs[12:20]
    in_part, out_part, back_part, gu_hbm, down_hbm = refs[20:25]
    plane_acts, small_ref, init_ref = refs[25:28], refs[28], refs[29]
    own_gu, own_down, far_gu, far_down, in_all, out_all = refs[30:36]
    core_got, back_got, back_own, small_out, gains_out, init_out = refs[36:42]
    x_all, o_all, act, d_gate, d_up, gu_ref, down_ref, slots = refs[42:50]
    back_low, back_load, small_got, gains_got, init_got = refs[50:55]
    in_bufs, out_bufs = refs[55:61], refs[61:67]
    load_sems, sum_sems, tile_send, tile_recv, phase_send, phase_recv = refs[67:]
    step = pl.program_id(0)
    rows, width = x_all.shape
    me = lax.axis_index("head")
    chip, core = me // 2, lax.rem(me, 2)
    member = lax.axis_index("mlp")
    partner = core_peer()
    near = near_peers()
    across, along = near[0], near[1]
    others = [head_peer(ahead) for ahead in range(1, 8)]
    hidden = own_gu.shape[1]
    sides = ((in_part, in_all, in_bufs), (out_part, out_all, out_bufs))

    def piece(part, of_member, half):
        size = part.shape[0] // 8
        return part.at[pl.ds(pl.multiple_of(of_member * 2 * size + half * size, size), size)]

    def quick_moves():
        moves = [(back_part.at[:, 1 - core], core_got, partner)]
        for at in range(3):
            moves.append((small_ref, small_got.at[at], near[at]))
            moves.append((init_ref, init_got.at[at], near[at]))
        return moves

    def line_sums():
        moves = [(back_low.at[chip], back_own, None)]
        for hops in range(1, 4):
            moves.append(
                (back_low.at[lax.rem(chip + hops, 4)], back_got.at[hops - 1], chip_peer(hops))
            )
        gains = small_out.at[pl.ds(0, 8)]
        return moves + [(gains, gains_got.at[at], others[at]) for at in range(7)]

    def reduce_one():
        moves = []
        for part, _, (got, _, _, _, _, _) in sides:
            moves.append((piece(part, near[0]["mlp"], 0), got.at[0], across))
            moves.append((piece(part, near[2]["mlp"], 0), got.at[1], across))
            moves.append((piece(part, near[1]["mlp"], 1), got.at[2], along))
            moves.append((piece(part, near[2]["mlp"], 1), got.at[3], along))
        return moves

    def reduce_two():
        moves = []
        for _, _, (_, _, passed, _, got, _) in sides:
            moves += [(passed.at[0], got.at[0], along), (passed.at[1], got.at[1], across)]
        return moves

    def spread_one():
        moves = []
        for _, whole, (_, _, _, _, _, total) in sides:
            moves += [(total, whole.at[member], peer) for peer in (across, along, None)]
        return moves

    def spread_two():
        moves = []
        for _, whole, _ in sides:
            half = whole.shape[1] // 2
            top = whole.at[across["mlp"], pl.ds(0, half)]
            bottom = whole.at[along["mlp"], pl.ds(half, half)]
            moves += [(top, top, along), (bottom, bottom, across)]
        return moves

    phases = [quick_moves, line_sums, reduce_one, reduce_two, spread_one, spread_two]

    def begin(at):
        launch(phases[at](), phase_send.at[at], phase_recv.at[at])

    def end(at):
        settle(phases[at](), phase_send.at[at], phase_recv.at[at])

    near_rows = x_own.shape[0]
    plane_rows = 4 * near_rows
    piece_rows = (rows - plane_rows) // 8
    sizes = (UNITS, hidden - UNITS)

    def weight_moves(at):
        span, size = pl.ds(at * UNITS, sizes[at]), pl.ds(0, sizes[at])
        return [(gu_hbm.at[:, span], gu_ref.at[:, size]), (down_hbm.at[span], down_ref.at[size])]

    def act_moves(at):
        span, size = pl.ds(at * UNITS, sizes[at]), pl.ds(0, sizes[at])
        return [
            (part.at[span], whole.at[size, pl.ds(0, plane_rows)])
            for part, whole in zip(plane_acts, (act, d_gate, d_up))
        ]

    def far_moves(begin, end):
        moves = []
        for at in range(begin, end):
            place = pl.ds(plane_rows + at * piece_rows, piece_rows)
            moves += [(x_far[at], x_all.at[place]), (o_far[at], o_all.at[place])]
        return moves

    def near_moves():
        moves = []
        for own, got, whole in ((x_own, x_got, x_all), (o_own, o_got, o_all)):
            moves.append((own, whole.at[pl.ds(0, near_rows)]))
            for at in range(3):
                moves.append((got.at[at], whole.at[pl.ds((at + 1) * near_rows, near_rows)]))
        return moves

    groups = [far_moves(0, 3), far_moves(3, 6), far_moves(6, 8), near_moves()]
    bases = [5, 11, 17, 21]

    def loads(moves, base):
        return [
            pltpu.make_async_copy(source, target, load_sems.at[base + at])
            for at, (source, target) in enumerate(moves)
        ]

    def fetch(moves, base):
        for copy in loads(moves, base):
            copy.start()

    def fetched(moves, base):
        for copy in loads(moves, base):
            copy.wait()

    def chunk_moves(at, column):
        span, size = pl.ds(at * UNITS, sizes[at]), pl.ds(0, sizes[at])
        columns = pl.ds(pl.multiple_of(column * SPAN, SPAN), SPAN)
        slot = slots.at[lax.rem(column, 2)]
        moves = []
        for gu, down, peer in ((own_gu, own_down, None), (far_gu, far_down, partner)):
            moves += [
                (slot.at[0, size], gu.at[0, span, columns], peer),
                (slot.at[1, size], gu.at[1, span, columns], peer),
                (slot.at[2, size], down.at[span, columns], peer),
            ]
        return moves

    def chunk_sems(at, column):
        place = 4 * at + column
        return tile_send.at[place], tile_recv.at[place]

    @pl.when(step == 0)
    def _():
        fetch(weight_moves(0), 0)
        fetch(groups[0], bases[0])
        greet(near + others)
        begin(0)
        begin(2)
        for at in range(1, 4):
            fetch(groups[at], bases[at])
        fetch(act_moves(0), 2)
        fetched(weight_moves(0), 0)

    @pl.when(step == 1)
    def _():
        fetch(act_moves(1), 2)
        fetched(weight_moves(1), 0)

    def reduce_sums():
        parts = []
        for part, _, (_, own, _, _, _, _) in sides:
            parts.append((piece(part, member, 0), own.at[0]))
            parts.append((piece(part, near[1]["mlp"], 0), own.at[1]))
            parts.append((piece(part, member, 1), own.at[2]))
            parts.append((piece(part, near[0]["mlp"], 1), own.at[3]))
        gather_parts(parts, sum_sems)
        end(2)
        for _, _, (got, own, passed, kept, _, _) in sides:
            for half in range(2):
                kept[half] = own[2 * half].astype(F32) + got[2 * half].astype(F32)
                passed[half] = (
                    own[2 * half + 1].astype(F32) + got[2 * half + 1].astype(F32)
                ).astype(BF16)
        begin(3)

    def reduce_totals():
        end(3)
        for _, _, (_, _, _, kept, got, total) in sides:
            size = total.shape[0] // 2
            for half in range(2):
                total[pl.ds(half * size, size), :] = (kept[half] + got[half].astype(F32)).astype(BF16)
        begin(4)

    def spread_rest():
        end(4)
        begin(5)

    def line_totals():
        end(0)

        def add(at, _):
            gather_parts(
                [(core_got.at[at], back_load.at[0]), (back_part.at[at, core], back_load.at[1])],
                sum_sems,
            )
            back_low[at] = (back_load[0].astype(F32) + back_load[1].astype(F32)).astype(BF16)
            return 0

        lax.fori_loop(0, 4, add, 0)
        total, first = small_ref[...], init_ref[...]
        for at in range(3):
            total = total + small_got[at]
            first = first + init_got[at]
        small_out[...] = total
        init_out[...] = first
        begin(1)

    def ahead(at, _):
        for group in range(3):

            @pl.when(jnp.logical_and(step == 0, at == group))
            def _(group=group):
                fetched(groups[group], bases[group])

        pl.when(jnp.logical_and(step == 0, at == 1))(line_totals)
        pl.when(jnp.logical_and(step == 1, at == 1))(reduce_totals)
        span = pl.ds(pl.multiple_of(plane_rows + at * SPAN, SPAN), SPAN)
        rows_in = x_all[span, :]
        gate = mm_nt(gu_ref[0], rows_in)
        up = mm_nt(gu_ref[1], rows_in)
        d_act = mm_nt(down_ref[...], o_all[span, :])
        silu, slope = gated(gate, up)
        act[:, span] = (silu * up).astype(BF16)
        d_gate[:, span] = (d_act * up * slope).astype(BF16)
        d_up[:, span] = (d_act * silu).astype(BF16)
        return 0

    lax.fori_loop(0, (rows - plane_rows) // SPAN, ahead, 0)

    @pl.when(step == 0)
    def _():
        fetch(weight_moves(1), 0)
        fetched(groups[3], bases[3])
        fetched(act_moves(0), 2)

    @pl.when(step == 1)
    def _():
        fetched(act_moves(1), 2)

    def back(at, _):
        pl.when(jnp.logical_and(step == 0, at == 2))(reduce_sums)
        pl.when(jnp.logical_and(step == 1, at == 3))(spread_rest)

        for of_tile in range(2):

            @pl.when(jnp.logical_and(step == of_tile, at >= 2))
            def _(of_tile=of_tile):
                settle(chunk_moves(of_tile, at - 2), *chunk_sems(of_tile, at - 2))

        @pl.when(jnp.logical_and(step == 1, at < 2))
        def _():
            settle(chunk_moves(0, at + 2), *chunk_sems(0, at + 2))

        span = pl.ds(pl.multiple_of(at * SPAN, SPAN), SPAN)
        columns = x_all[:, span]
        slot = lax.rem(at, 2)
        slots[slot, 0] = mm(d_gate[...], columns).astype(BF16)
        slots[slot, 1] = mm(d_up[...], columns).astype(BF16)
        slots[slot, 2] = mm(act[...], o_all[:, span]).astype(BF16)

        for of_tile in range(2):

            @pl.when(step == of_tile)
            def _(of_tile=of_tile):
                launch(chunk_moves(of_tile, at), *chunk_sems(of_tile, at))

        return 0

    lax.fori_loop(0, width // SPAN, back, 0)

    @pl.when(step == 1)
    def _():
        end(1)
        gains = small_out[0:8, :]
        for at in range(7):
            gains = gains + gains_got[at]
        gains_out[...] = gains
        for at in (2, 3):
            settle(chunk_moves(1, at), *chunk_sems(1, at))
        end(5)


def reduce_buffers(part):
    size, width = part.shape[0] // 8, part.shape[1]
    return [
        pltpu.VMEM((4, size, width), BF16),
        pltpu.VMEM((4, size, width), BF16),
        pltpu.VMEM((2, size, width), BF16),
        pltpu.VMEM((2, size, width), F32),
        pltpu.VMEM((2, size, width), BF16),
        pltpu.VMEM((2 * size, width), BF16),
    ]


def mlp_grads(
    x, o, in_part, out_part, back_part, gate_up_rows, down_weight, plane_acts, small, init, collective_id
):
    arrays = [x[0], x[1], *x[2], o[0], o[1], *o[2], in_part, out_part, back_part]
    arrays += [gate_up_rows, down_weight, *plane_acts]
    hidden, width = down_weight.shape
    near = x[0].shape[0]
    rows = 16 * near
    vmem = pl.BlockSpec(memory_space=pltpu.VMEM)
    low = [
        (2, hidden, width),
        (hidden, width),
        (2, hidden, width),
        (hidden, width),
        (4, in_part.shape[0] // 4, in_part.shape[1]),
        (4, out_part.shape[0] // 4, width),
        (4, near, width),
        (3, near, width),
        (near, width),
    ]
    got = pl.pallas_call(
        grads_kernel,
        grid=(2,),
        in_specs=anywhere(len(arrays)) + [vmem, vmem],
        out_specs=anywhere(len(low)) + [vmem, vmem, vmem],
        out_shape=[jax.ShapeDtypeStruct(shape, BF16) for shape in low]
        + [
            jax.ShapeDtypeStruct(small.shape, F32),
            jax.ShapeDtypeStruct((8, width), F32),
            jax.ShapeDtypeStruct(init.shape, F32),
        ],
        scratch_shapes=[
            pltpu.VMEM((rows, width), BF16),
            pltpu.VMEM((rows, width), BF16),
            pltpu.VMEM((UNITS, rows), BF16),
            pltpu.VMEM((UNITS, rows), BF16),
            pltpu.VMEM((UNITS, rows), BF16),
            pltpu.VMEM((2, UNITS, width), BF16),
            pltpu.VMEM((UNITS, width), BF16),
            pltpu.VMEM((2, 3, UNITS, SPAN), BF16),
            pltpu.VMEM((4, near, width), BF16),
            pltpu.VMEM((2, near, width), BF16),
            pltpu.VMEM((3, *small.shape), F32),
            pltpu.VMEM((7, 8, width), F32),
            pltpu.VMEM((3, *init.shape), F32),
            *reduce_buffers(in_part),
            *reduce_buffers(out_part),
            pltpu.SemaphoreType.DMA((29,)),
            pltpu.SemaphoreType.DMA((8,)),
            pltpu.SemaphoreType.DMA((8, 6)),
            pltpu.SemaphoreType.DMA((8, 6)),
            pltpu.SemaphoreType.DMA((6, 11)),
            pltpu.SemaphoreType.DMA((6, 11)),
        ],
        compiler_params=pltpu.CompilerParams(
            vmem_limit_bytes=VMEM_MOST, collective_id=collective_id, has_side_effects=True
        ),
        cost_estimate=pl.CostEstimate(
            flops=11 * rows * hidden * width, bytes_accessed=14 * hidden * width, transcendentals=rows * hidden
        ),
        name="mlp_grads",
    )(*arrays, small, init)
    return got[:6], got[7], got[8], got[9], got[10], got[11]


def dots_kernel(*refs):
    dproj, columns, weight, rate, first_gain, mlp_part, dgain, dbias = refs[:8]
    side_a, side_b, in_part, back_part, small, corner_a, corner_b, send, recv = refs[8:]
    step = pl.program_id(0)
    wide = weight.shape[1]
    near = near_peers()[:2]
    moves = [(side_a, corner_a, near[1]), (side_b, corner_b, near[0])]

    @pl.when(step == 0)
    def _():
        greet(near)
        launch(moves, send, recv)

    in_part[...] = mm_tn(columns[...], dproj[:, :wide]).astype(BF16)
    rates = mm_tn(dproj[:, wide:], columns[...])
    back = mm_nt(dproj[:, :wide], weight[...]) + mm(dproj[:, wide:], rate[...])
    back_part[...] = back.astype(BF16)
    gains = jnp.sum(back * columns[...].astype(F32), axis=0, keepdims=True)
    small[...] = jnp.zeros_like(small)
    small[8:16, :] = rates[:8]
    small[0:1, :] = gains / first_gain[...]
    small[1:2, :] = mlp_part[...]

    @pl.when(step == 0)
    def _():
        small[2:3, : dgain.shape[1]] = dgain[...]
        small[2:3, dgain.shape[1] : 2 * dgain.shape[1]] = dbias[...]

    @pl.when(step == pl.num_programs(0) - 1)
    def _():
        settle(moves, send, recv)


def dots(dproj, gathered, weight, rate, gains, mlp_part, dgain, dbias, side_a, side_b, collective_id):
    rows, width = gathered.shape
    full = lambda *shape: pl.BlockSpec(shape, lambda i: (0,) * len(shape))
    cols = lambda height: pl.BlockSpec((height, SPAN), lambda i: (0, i))
    down = lambda wide: pl.BlockSpec((SPAN, wide), lambda i: (i, 0))
    return pl.pallas_call(
        dots_kernel,
        grid=(width // SPAN,),
        in_specs=[
            full(*dproj.shape),
            cols(rows),
            down(weight.shape[1]),
            cols(rate.shape[0]),
            cols(1),
            cols(1),
            full(*dgain.shape),
            full(*dbias.shape),
            *anywhere(2),
        ],
        out_specs=[down(weight.shape[1]), cols(rows), cols(16), *anywhere(2)],
        out_shape=[
            jax.ShapeDtypeStruct(weight.shape, BF16),
            jax.ShapeDtypeStruct((rows, width), BF16),
            jax.ShapeDtypeStruct((16, width), F32),
            *[jax.ShapeDtypeStruct(side_a.shape, BF16)] * 2,
        ],
        scratch_shapes=sem_pair(2),
        compiler_params=pltpu.CompilerParams(
            vmem_limit_bytes=VMEM_MOST, collective_id=collective_id, has_side_effects=True
        ),
        cost_estimate=pl.CostEstimate(
            flops=4 * rows * width * dproj.shape[1], bytes_accessed=24 * 1024 * 1024, transcendentals=0
        ),
        name="dots",
    )(dproj, gathered, weight, rate, gains, mlp_part, dgain, dbias, side_a, side_b)


def finish_kernel(*refs):
    own_gu, far_gu, own_down, far_down, in_ref, out_ref = refs[:6]
    tokens, hidden, d_hidden, gain, plane_total, back_own, back_got = refs[6:13]
    small, sums, init_in = refs[13:16]
    gu, down, in_out, out_out, result, d_tokens = refs[16:22]
    first, second, mix_gain, mix_bias, d_rate, d_init = refs[22:]

    @pl.when(pl.program_id(0) == 0)
    def _():
        local = mix_gain.shape[1]
        first[...] = sums[0:1, :]
        second[...] = sums[1:2, :]
        mix_gain[...] = small[2:3, :local]
        mix_bias[...] = small[2:3, local : 2 * local]
        d_rate[...] = small[8 : 8 + d_rate.shape[0], :]
        d_init[...] = init_in[...]

    gu[...] = own_gu[...].astype(F32) + far_gu[...].astype(F32)
    down[...] = own_down[...].astype(F32) + far_down[...].astype(F32)
    width = in_out.shape[2]
    for part in range(4):
        in_out[:, part, :] = in_ref[:, part * width : (part + 1) * width].astype(F32)
    out_out[...] = out_ref[...].astype(F32)
    d_normed = back_own[...].astype(F32)
    for at in range(3):
        d_normed = d_normed + back_got[at].astype(F32)
    result[...] = (hidden[...] + plane_total[...]).astype(BF16)
    source = tokens[...].astype(F32)
    d_tokens[...] = d_hidden[...] + norm_back(source, rms_scale(source), gain[...], d_normed)


def finish(own_gu, far_gu, own_down, far_down, in_all, out_all, tokens, hidden, d_hidden, gain, plane_total, backs, small, sums, init, local):
    units, width = own_down.shape
    tall, wide = in_all.shape
    near = tokens.shape[0]
    steps = pl.cdiv(units, FINISH)
    rows = lambda *shape: pl.BlockSpec(shape, lambda i: (i,) + (0,) * (len(shape) - 1))
    few = near // steps
    full = lambda *shape: pl.BlockSpec(shape, lambda i: (0,) * len(shape))
    little = [(1, width), (1, width), (1, local), (1, local), (init.shape[0], width), init.shape]
    return pl.pallas_call(
        finish_kernel,
        grid=(steps,),
        in_specs=[tile(2, FINISH, width)] * 2
        + [tile(FINISH, width)] * 2
        + [rows(tall // steps, wide), rows(out_all.shape[0] // steps, width)]
        + [rows(few, width)] * 3
        + [pl.BlockSpec((1, width), lambda i: (0, 0)), rows(few, width)]
        + [rows(few, width), tile(3, few, width)]
        + [full(*small.shape), full(*sums.shape), full(*init.shape)],
        out_specs=[
            tile(2, FINISH, width),
            tile(FINISH, width),
            rows(tall // steps, 4, wide // 4),
            rows(out_all.shape[0] // steps, width),
            rows(few, width),
            rows(few, width),
            *[full(*shape) for shape in little],
        ],
        out_shape=[
            jax.ShapeDtypeStruct((2, units, width), F32),
            jax.ShapeDtypeStruct((units, width), F32),
            jax.ShapeDtypeStruct((tall, 4, wide // 4), F32),
            jax.ShapeDtypeStruct(out_all.shape, F32),
            jax.ShapeDtypeStruct((near, width), BF16),
            jax.ShapeDtypeStruct((near, width), F32),
            *[jax.ShapeDtypeStruct(shape, F32) for shape in little],
        ],
        compiler_params=pltpu.CompilerParams(vmem_limit_bytes=VMEM_MOST),
        cost_estimate=pl.CostEstimate(
            flops=3 * units * width, bytes_accessed=24 * units * width, transcendentals=0
        ),
        name="finish",
    )(own_gu, far_gu, own_down, far_down, in_all, out_all, tokens, hidden, d_hidden, gain, plane_total, *backs, small, sums, init)


PIECE = 2048


def rms_scale(values):
    return lax.rsqrt(jnp.mean(values * values, axis=-1, keepdims=True) + 1e-06)


def norm_back(values, row_scale, gains, upstream):
    weighted = upstream * gains
    return row_scale * weighted - values * row_scale**3 * jnp.mean(
        weighted * values, axis=-1, keepdims=True
    )


def contract_rows(left, right):
    return lax.dot_general(
        left, right, (((0,), (0,)), ((), ())), preferred_element_type=jnp.float32
    )


def contract_cols(left, right):
    return lax.dot_general(
        left, right, (((1,), (1,)), ((), ())), preferred_element_type=jnp.float32
    )


def after(values, *others):
    return lax.optimization_barrier((values, *others))[0]


def swap_core(values):
    size = lax.axis_size("head")
    return lax.ppermute(values, "head", [(at, at ^ 1) for at in range(size)])


def shift_chip(values, hops):
    size = lax.axis_size("head")
    return lax.ppermute(values, "head", [(at, (at + 2 * hops) % size) for at in range(size)])


def swap_mlp(values, flip):
    size = lax.axis_size("mlp")
    return lax.ppermute(values, "mlp", [(at, at ^ flip) for at in range(size)])


def sum_small(values, axis):
    size = lax.axis_size(axis)
    flip = 1
    while flip < size:
        values = values + lax.ppermute(values, axis, [(at, at ^ flip) for at in range(size)])
        flip *= 2
    return values


def spread_mlp(values):
    return [values] + [swap_mlp(values, flip) for flip in range(1, lax.axis_size("mlp"))]


def scatter_mlp(parts):
    total = parts[0]
    for flip in range(1, len(parts)):
        total = total + swap_mlp(parts[flip].astype(BF16), flip).astype(F32)
    return total


def sum_mlp(values, shape):
    size = lax.axis_size("mlp")
    me = lax.axis_index("mlp")
    rows = values.shape[0] // size
    low = values.astype(BF16)
    total = lax.dynamic_slice_in_dim(values, me * rows, rows)
    for flip in range(1, size):
        part = lax.dynamic_slice_in_dim(low, (me ^ flip) * rows, rows)
        total = total + swap_mlp(part, flip).astype(F32)
    own = total.astype(BF16)
    whole = jnp.zeros((values.shape[0],) + shape, F32)
    start = (0,) * len(shape)
    whole = lax.dynamic_update_slice(whole, total.reshape((rows,) + shape), (me * rows,) + start)
    for flip in range(1, size):
        part = swap_mlp(own, flip).astype(F32).reshape((rows,) + shape)
        whole = lax.dynamic_update_slice(whole, part, ((me ^ flip) * rows,) + start)
    return whole


def on_device(
    tokens,
    out_grad,
    seq_lengths,
    norm_gain,
    in_weight,
    rate_weight,
    init_state,
    mix_gain,
    mix_bias,
    out_weight,
    mlp_gain,
    gate_up,
    down_weight,
):
    core = lax.axis_index("head") % 2
    chips = lax.axis_size("head") // 2
    row_total = tokens.shape[1]
    model_width = tokens.shape[2]
    local_width = in_weight.shape[2]
    head_count = init_state.shape[0]
    first_gain = norm_gain.astype(jnp.float32)
    second_gain = mlp_gain.astype(jnp.float32)
    source = tokens[0].astype(jnp.float32)
    cotangent = out_grad[0]
    first_scale = rms_scale(source)
    normed = (source * first_scale * first_gain).astype(BF16)
    gathered = lax.all_gather(normed, "head", axis=0, tiled=True)
    in_flat = jnp.concatenate(
        [
            in_weight.reshape(model_width, 4 * local_width),
            rate_weight,
            jnp.zeros((model_width, LANES - head_count), BF16),
        ],
        axis=1,
    )
    cot_plane = spread_mlp(cotangent)
    projected = jnp.dot(gathered, in_flat, preferred_element_type=jnp.float32)
    mix_gains = mix_gain.astype(jnp.float32)[None]
    mix_biases = mix_bias.astype(jnp.float32)[None]
    (mixed, *kept), _ = mixer_forward(
        seq_lengths, projected, init_state, mix_gains, mix_biases, Carry()
    )

    late_out_weight, late_cotangent, _ = lax.optimization_barrier((out_weight, cotangent, gathered))
    out_full = lax.all_gather(late_out_weight, "head", axis=0, tiled=True)
    cot_far = [shift_chip(late_cotangent, hops) for hops in range(1, chips)]
    cot_far = jnp.concatenate(cot_far, axis=0)
    cot_all = jnp.concatenate(cot_plane + spread_mlp(cot_far), axis=0)
    cot_plane = jnp.concatenate(cot_plane, axis=0)

    mixed_rows = lax.all_to_all(mixed, "head", 0, 1, tiled=True)
    branch = jnp.dot(mixed_rows, out_full, preferred_element_type=jnp.float32)
    hidden = source + branch
    second_scale = rms_scale(hidden)
    normed2 = (hidden * second_scale * second_gain).astype(BF16)

    gate_up_rows = jnp.transpose(gate_up, (1, 2, 0))
    gate_rows, up_rows = gate_up_rows[0], gate_up_rows[1]
    normed_plane = spread_mlp(normed2)
    normed_far = [shift_chip(normed2, hops) for hops in range(1, chips)]
    plane = jnp.concatenate(normed_plane, axis=0)
    gate = contract_cols(plane, gate_rows)
    up = contract_cols(plane, up_rows)
    silu, slope = gated(gate, up)
    d_act = contract_cols(cot_plane, down_weight)
    d_gate = (d_act * up * slope).astype(BF16)
    d_up = (d_act * silu).astype(BF16)
    d_plane = jnp.dot(d_gate, gate_rows, preferred_element_type=jnp.float32) + jnp.dot(
        d_up, up_rows, preferred_element_type=jnp.float32
    )
    members = lax.axis_size("mlp")
    d_normed2 = scatter_mlp([d_plane[at * row_total : (at + 1) * row_total] for at in range(members)])
    activation = (silu * up).astype(BF16)
    out_plane = jnp.dot(activation, down_weight, preferred_element_type=jnp.float32)
    mlp_out = scatter_mlp([out_plane[at * row_total : (at + 1) * row_total] for at in range(members)])
    result = (hidden + mlp_out).astype(BF16)[None]

    grad_mlp_gain = sum_small(
        sum_small(jnp.sum(d_normed2 * hidden * second_scale, axis=0), "mlp"), "head"
    )
    d_hidden = cotangent.astype(jnp.float32) + norm_back(
        hidden, second_scale, second_gain, d_normed2
    )
    d_branch = d_hidden.astype(BF16)
    d_mixed_rows = contract_cols(d_branch, out_full).astype(BF16)
    d_mixed = lax.all_to_all(d_mixed_rows, "head", 1, 0, tiled=True)
    shard_rows = lax.all_gather(d_branch, "head", axis=0, tiled=True)
    (d_projected, grad_init_state, grad_mix_gain, grad_mix_bias), _ = mixer_backward(
        seq_lengths, d_mixed, projected, init_state, mix_gains, mix_biases, kept, Carry()
    )
    grad_in_flat = contract_rows(gathered, d_projected)
    grad_in_weight = sum_mlp(grad_in_flat[:, : 4 * local_width], (4, local_width))
    d_normed = lax.psum_scatter(
        contract_cols(d_projected, in_flat).astype(BF16),
        "head",
        scatter_dimension=0,
        tiled=True,
    ).astype(jnp.float32)
    grad_out_weight = sum_mlp(contract_rows(mixed, shard_rows), (model_width,))
    small = jnp.concatenate(
        [
            grad_in_flat[:, 4 * local_width : 4 * local_width + head_count].reshape(-1),
            grad_init_state.reshape(-1),
            grad_mix_gain[0],
            grad_mix_bias[0],
        ]
    )
    small = sum_small(small, "mlp")
    sizes = [model_width * head_count, grad_init_state.size, local_width, local_width]
    ends = [sum(sizes[: at + 1]) for at in range(4)]
    grad_rate_weight = small[: ends[0]].reshape(model_width, head_count)
    grad_init_state = small[ends[0] : ends[1]].reshape(grad_init_state.shape)
    grad_mix_gain = small[ends[1] : ends[2]]
    grad_mix_bias = small[ends[2] : ends[3]]
    grad_norm_gain = sum_small(
        sum_small(jnp.sum(d_normed * source * first_scale, axis=0), "mlp"), "head"
    )
    grad_tokens = d_hidden + norm_back(source, first_scale, first_gain, d_normed)

    far, _ = lax.optimization_barrier((jnp.concatenate(normed_far, axis=0), d_normed2))
    normed_all = jnp.concatenate(normed_plane + spread_mlp(far), axis=0)
    half = model_width // 2
    pieces = max(1, normed_all.shape[0] // PIECE)
    piece = normed_all.shape[0] // pieces
    sums = None
    for at in range(pieces):
        rows_in = normed_all[at * piece : (at + 1) * piece]
        rows_cot = cot_all[at * piece : (at + 1) * piece]
        if sums is not None:
            rows_in, rows_cot, sums = lax.optimization_barrier((rows_in, rows_cot, sums))
        gate = contract_cols(rows_in, gate_rows)
        up = contract_cols(rows_in, up_rows)
        silu, slope = gated(gate, up)
        activation = (silu * up).astype(BF16)
        d_act = contract_cols(rows_cot, down_weight)
        d_gate = d_act * up * slope
        d_up = d_act * silu
        mine = jnp.where(core == 0, d_gate, d_up).astype(BF16)
        theirs = jnp.where(core == 0, d_up, d_gate).astype(BF16)
        cot_theirs = jnp.where(core == 0, rows_cot[:, half:], rows_cot[:, :half])
        cot_mine = jnp.where(core == 0, rows_cot[:, :half], rows_cot[:, half:])
        terms = [
            contract_rows(theirs, rows_in),
            contract_rows(activation, cot_theirs),
            contract_rows(mine, rows_in),
            contract_rows(activation, cot_mine),
        ]
        sums = terms if sums is None else [old + new for old, new in zip(sums, terms)]
    gate_theirs = swap_core(sums[0].astype(BF16))
    down_theirs = swap_core(sums[1].astype(BF16))
    gate_mine = sums[2] + gate_theirs.astype(F32)
    down_mine = sums[3] + down_theirs.astype(F32)
    gate_other = swap_core(gate_mine.astype(BF16)).astype(F32)
    down_other = swap_core(down_mine.astype(BF16)).astype(F32)
    grad_gate_up = jnp.stack(
        [jnp.where(core == 0, gate_mine, gate_other), jnp.where(core == 0, gate_other, gate_mine)]
    )
    grad_gate_up = jnp.transpose(grad_gate_up, (2, 0, 1))
    grad_down = jnp.concatenate(
        [jnp.where(core == 0, down_mine, down_other), jnp.where(core == 0, down_other, down_mine)],
        axis=1,
    )
    return (
        result,
        grad_tokens[None],
        grad_norm_gain,
        grad_in_weight,
        grad_rate_weight,
        grad_init_state,
        grad_mix_gain,
        grad_mix_bias,
        grad_out_weight,
        grad_mlp_gain,
        grad_gate_up,
        grad_down,
    )


def spread_kernel(*refs):
    mixed_rows, tokens, gain, out_cross, out_other, cot, cot_line = refs[:7]
    hidden, normed2, got, line, side_x, side_y = refs[7:13]
    weights, loads, send, recv = refs[13:]
    across, along = near_peers()[:2]
    half = tokens.shape[0] // 2
    top, bottom = pl.ds(0, half), pl.ds(half, half)
    direct = [(normed2, got.at[0], across), (normed2, got.at[1], along)]
    corner = [
        (got.at[0, top], got.at[2, top], along),
        (got.at[1, bottom], got.at[2, bottom], across),
    ]
    rest = line_moves(cot, 1, line) + [(cot_line, side_x, across), (cot_line, side_y, along)]
    fetch = [
        pltpu.make_async_copy(part, weights.at[at], loads.at[at])
        for at, part in enumerate((out_cross, out_other))
    ]
    for copy in fetch:
        copy.start()
    greet([across, along, *line_peers()])
    launch(rest, send.at[2], recv.at[2])
    for copy in fetch:
        copy.wait()

    def body(at, _):
        span = pl.ds(pl.multiple_of(at * SPAN, SPAN), SPAN)
        branch = mm(mixed_rows[0], weights[0, :, span]) + mm(mixed_rows[1], weights[1, :, span])
        hidden[:, span] = tokens[:, span].astype(F32) + branch
        return 0

    lax.fori_loop(0, tokens.shape[1] // SPAN, body, 0)
    values = hidden[...]
    normed2[...] = (values * rms_scale(values) * gain[:, values.shape[1] : 2 * values.shape[1]]).astype(BF16)
    launch(direct, send.at[0], recv.at[0])
    settle(direct, send.at[0], recv.at[0])
    launch(corner, send.at[1], recv.at[1])
    settle(corner, send.at[1], recv.at[1])
    settle(rest, send.at[2], recv.at[2])


def spread_plane(mixed_rows, tokens, gains, out_halves, cot, cot_line, collective_id):
    rows, width = tokens.shape
    vmem = pl.BlockSpec(memory_space=pltpu.VMEM)
    return pl.pallas_call(
        spread_kernel,
        in_specs=[vmem, vmem, vmem, *anywhere(4)],
        out_specs=[vmem, vmem, *anywhere(4)],
        out_shape=[
            jax.ShapeDtypeStruct((rows, width), F32),
            jax.ShapeDtypeStruct((rows, width), BF16),
            jax.ShapeDtypeStruct((3, rows, width), BF16),
            *[jax.ShapeDtypeStruct((3 * rows // 2, width), BF16)] * 3,
        ],
        scratch_shapes=[
            pltpu.VMEM((2, width // 2, width), BF16),
            pltpu.SemaphoreType.DMA((2,)),
            pltpu.SemaphoreType.DMA((3, 5)),
            pltpu.SemaphoreType.DMA((3, 5)),
        ],
        compiler_params=pltpu.CompilerParams(
            vmem_limit_bytes=VMEM_MOST, collective_id=collective_id, has_side_effects=True
        ),
        cost_estimate=pl.CostEstimate(
            flops=2 * rows * width * width, bytes_accessed=3 * width * width, transcendentals=0
        ),
        name="spread_plane",
    )(mixed_rows, tokens, gains, *out_halves, cot, cot_line)


class PlaneSum:
    def __init__(self, parts, bufs, send, recv, loads):
        self.parts = parts
        self.got, self.own, self.passed, self.kept, self.late = bufs
        self.send, self.recv, self.loads = send, recv, loads
        self.across, self.along = near_peers()[:2]
        half = parts.shape[1] // 2
        self.spans = (pl.ds(0, half), pl.ds(half, half))

    def moves(self, phase):
        top, bottom = self.spans
        if phase == 0:
            return [
                (self.parts.at[1, top], self.got.at[0], self.across),
                (self.parts.at[3, top], self.got.at[1], self.across),
                (self.parts.at[2, bottom], self.got.at[2], self.along),
                (self.parts.at[3, bottom], self.got.at[3], self.along),
            ]
        return [
            (self.passed.at[0], self.late.at[0], self.along),
            (self.passed.at[1], self.late.at[1], self.across),
        ]

    def begin(self):
        launch(self.moves(0), self.send.at[0], self.recv.at[0])

    def middle(self):
        top, bottom = self.spans
        gather_parts(
            [
                (self.parts.at[0, top], self.own.at[0]),
                (self.parts.at[2, top], self.own.at[1]),
                (self.parts.at[0, bottom], self.own.at[2]),
                (self.parts.at[1, bottom], self.own.at[3]),
            ],
            self.loads,
        )
        settle(self.moves(0), self.send.at[0], self.recv.at[0])
        for half in range(2):
            self.passed[half] = (
                self.own[2 * half + 1].astype(F32) + self.got[2 * half + 1].astype(F32)
            ).astype(BF16)
        launch(self.moves(1), self.send.at[1], self.recv.at[1])
        for half in range(2):
            self.kept[half] = self.own[2 * half].astype(F32) + self.got[2 * half].astype(F32)

    def finish(self, target):
        settle(self.moves(1), self.send.at[1], self.recv.at[1])
        for half in range(2):
            target[self.spans[half], :] = self.kept[half] + self.late[half].astype(F32)


def plane_buffers(rows, width):
    half = rows // 2
    return [
        pltpu.VMEM((4, half, width), BF16),
        pltpu.VMEM((4, half, width), BF16),
        pltpu.VMEM((2, half, width), BF16),
        pltpu.VMEM((2, half, width), F32),
        pltpu.VMEM((2, half, width), BF16),
    ]


def turn_kernel(*refs):
    d_plane, out_plane, normed2, out_cross, out_other, hidden, cot, gain = refs[:8]
    d_mixed, line, d_hidden, d_branch, mlp_part, plane_total = refs[8:14]
    d_bufs, out_bufs, weights, slots, d_normed = refs[14:19], refs[19:24], refs[24], refs[25], refs[26]
    sum_send, sum_recv, loads, row_send, row_recv, line_send, line_recv = refs[27:]
    me = lax.axis_index("head")
    chip, core = me // 2, lax.rem(me, 2)
    rows = hidden.shape[0]
    width = slots.shape[2]
    d_sum = PlaneSum(d_plane, d_bufs, sum_send.at[0], sum_recv.at[0], loads)
    out_sum = PlaneSum(out_plane, out_bufs, sum_send.at[1], sum_recv.at[1], loads)
    line_copies = line_moves(normed2, 1, line)
    fetch = [
        pltpu.make_async_copy(part, weights.at[at], loads.at[4 + at])
        for at, part in enumerate((out_cross, out_other))
    ]
    greet([d_sum.across, d_sum.along] + [head_peer(at) for at in range(1, 8)])
    d_sum.begin()
    launch(line_copies, line_send, line_recv)
    for copy in fetch:
        copy.start()
    d_sum.middle()
    d_sum.finish(d_normed)
    out_sum.begin()
    scale = rms_scale(hidden[...])
    part = d_normed[...]
    mlp_part[...] = jnp.sum(part * hidden[...] * scale, axis=0, keepdims=True)
    gains = gain[:, part.shape[1] : 2 * part.shape[1]]
    total = cot[...].astype(F32) + norm_back(hidden[...], scale, gains, part)
    d_hidden[...] = total
    d_branch[...] = total.astype(BF16)
    for copy in fetch:
        copy.wait()

    def row_copy(at, ahead, sender, target, local):
        place = d_mixed.at[pl.ds(pl.multiple_of(me * rows, rows), rows)]
        if local:
            return pltpu.make_async_copy(slots.at[at], place, row_send.at[at])
        return pltpu.make_async_remote_copy(
            src_ref=slots.at[at],
            dst_ref=place,
            send_sem=row_send.at[at],
            recv_sem=row_recv.at[ahead],
            device_id={"head": target},
            device_id_type=MESH,
        )

    order = (4, 3, 5, 2, 6, 1, 7, 0)
    for at, ahead in enumerate(order):
        target = lax.rem(me + ahead, 8)
        columns = pl.ds(pl.multiple_of(target // 2 * width, width), width)
        slots[at] = mm_nt(d_branch[...], weights[ahead % 2, columns, :]).astype(BF16)
        row_copy(at, ahead, me, target, ahead == 0).start()
    out_sum.middle()
    for at, ahead in enumerate(order):
        copy = row_copy(at, ahead, me, lax.rem(me + ahead, 8), ahead == 0)
        copy.wait()
    out_sum.finish(plane_total)
    settle(line_copies, line_send, line_recv)


def turn(d_plane, out_plane, normed2, out_halves, hidden, cot, gains, local_width, collective_id):
    rows, width = normed2.shape
    vmem = pl.BlockSpec(memory_space=pltpu.VMEM)
    return pl.pallas_call(
        turn_kernel,
        in_specs=anywhere(5) + [vmem] * 3,
        out_specs=anywhere(2) + [vmem] * 4,
        out_shape=[
            jax.ShapeDtypeStruct((8 * rows, local_width), BF16),
            jax.ShapeDtypeStruct((3 * rows // 2, width), BF16),
            jax.ShapeDtypeStruct((rows, width), F32),
            jax.ShapeDtypeStruct((rows, width), BF16),
            jax.ShapeDtypeStruct((1, width), F32),
            jax.ShapeDtypeStruct((rows, width), F32),
        ],
        scratch_shapes=[
            *plane_buffers(rows, width),
            *plane_buffers(rows, width),
            pltpu.VMEM((2, width // 2, width), BF16),
            pltpu.VMEM((8, rows, local_width), BF16),
            pltpu.VMEM((rows, width), F32),
            pltpu.SemaphoreType.DMA((2, 2, 4)),
            pltpu.SemaphoreType.DMA((2, 2, 4)),
            pltpu.SemaphoreType.DMA((6,)),
            *sem_pair(8),
            *sem_pair(3),
        ],
        compiler_params=pltpu.CompilerParams(
            vmem_limit_bytes=VMEM_MOST, collective_id=collective_id, has_side_effects=True
        ),
        cost_estimate=pl.CostEstimate(
            flops=2 * rows * width * width, bytes_accessed=4 * width * width, transcendentals=0
        ),
        name="turn",
    )(d_plane, out_plane, normed2, *out_halves, hidden, cot, gains)


def halves_of(values):
    half = values.shape[0] // 2
    return pl.ds(0, half), pl.ds(half, half)


def sides_and_line(ins, outs):
    across, along = near_peers()[:2]
    top, bottom = halves_of(outs[2])
    moves = [
        (ins[0], outs[0], across),
        (ins[0], outs[1], along),
        (ins[1].at[top], outs[2].at[top], along),
        (ins[2].at[bottom], outs[2].at[bottom], across),
    ]
    return [across, along, *line_peers()], moves + line_moves(ins[3], 0, outs[4])


def corner_rest(ins, outs):
    across, along = near_peers()[:2]
    top, bottom = halves_of(outs[3])
    return [
        (outs[0].at[top], outs[3].at[top], along),
        (outs[1].at[bottom], outs[3].at[bottom], across),
    ]


def sides(ins, outs):
    near = near_peers()[:2]
    return near, [(ins[at // 2], outs[at], near[at % 2]) for at in range(4)]


def on_square(
    tokens,
    out_grad,
    seq_lengths,
    norm_gain,
    in_weight,
    rate_weight,
    init_state,
    mix_gain,
    mix_bias,
    out_weight,
    mlp_gain,
    gate_up,
    down_weight,
):
    heads = lax.axis_size("head")
    rows = tokens.shape[1]
    model_width = tokens.shape[2]
    local_width = in_weight.shape[2]
    head_count = init_state.shape[0]
    vectors = [part.reshape(-1, LANES) for part in (norm_gain, mlp_gain, mix_gain, mix_bias)]
    source = tokens[0]
    cotangent = out_grad[0]
    far_shape = (3 * rows // 2, model_width)
    (projected, rate_rows), (mixed, *kept), gains, moved = head(
        seq_lengths, source, rate_weight.T, init_state, vectors, in_weight, cotangent, out_weight, 0
    )
    gathered, cot_got, in_main, mixed_rows, out_cross, out_other, cot_line_a = moved
    out_halves = [part.reshape(model_width // 2, model_width) for part in (out_cross, out_other)]
    hidden, normed2, normed_got, cot_line_b, cot_x_a, cot_y_a = spread_plane(
        mixed_rows, source, gains, out_halves, cotangent, cot_line_a, 3
    )
    gate_up_rows = jnp.transpose(gate_up, (1, 2, 0))
    (d_plane, out_plane), plane_acts, moved = mlp_plane(
        normed2,
        normed_got,
        cotangent,
        cot_got,
        gate_up_rows,
        down_weight,
        Carry(
            [cot_line_b, cot_x_a, cot_y_a, normed2],
            [far_shape] * 5,
            sides_and_line,
            9,
            4,
            (1, 2, corner_rest),
        ),
    )
    cot_x_b, cot_y_b, cot_corner_a, cot_corner_b, normed_line_a = moved
    d_mixed, normed_line_b, d_hidden, d_branch, mlp_part, plane_total = turn(
        d_plane,
        out_plane,
        normed2,
        out_halves,
        hidden,
        cotangent,
        gains,
        local_width,
        5,
    )
    shard_rows = lax.all_gather(after(d_branch, d_mixed), "head", axis=0, tiled=True)
    (d_projected, grad_init_state, grad_mix_gain, grad_mix_bias), normed_sides = mixer_backward(
        seq_lengths,
        d_mixed,
        projected,
        init_state,
        gains,
        gains,
        kept,
        Carry([normed_line_a, normed_line_b], [far_shape] * 4, sides, 4, 7),
        (2 * model_width // local_width, 2 * model_width // local_width + 1),
    )
    in_part, back_part, small, normed_corner_a, normed_corner_b = dots(
        d_projected,
        gathered,
        in_main,
        rate_rows,
        gains,
        mlp_part,
        grad_mix_gain,
        grad_mix_bias,
        normed_sides[0],
        normed_sides[3],
        8,
    )
    out_part = contract_rows(mixed, after(shard_rows, in_part)).astype(BF16)
    cot_far = [cot_line_a, cot_line_b, cot_x_a, cot_x_b, cot_y_a, cot_y_b]
    normed_far = [normed_line_a, normed_line_b]
    normed_far += [normed_sides[0], normed_sides[2], normed_sides[1], normed_sides[3]]
    grads, back_got, back_own, small, sums, grad_init_state = mlp_grads(
        (normed2, normed_got, [*normed_far, normed_corner_a, normed_corner_b]),
        (cotangent, cot_got, [*cot_far, cot_corner_a, cot_corner_b]),
        in_part,
        out_part,
        back_part.reshape(heads // 2, 2, rows, model_width),
        gate_up_rows,
        down_weight,
        plane_acts,
        small,
        grad_init_state,
        9,
    )
    own_gate_up, own_down, other_gate_up, other_down, in_all, out_all = grads
    done = finish(
        own_gate_up,
        other_gate_up,
        own_down,
        other_down,
        in_all.reshape(in_main.shape),
        out_all.reshape(out_weight.shape),
        tokens[0],
        hidden,
        d_hidden,
        gains,
        plane_total,
        (back_own, back_got),
        small,
        sums,
        grad_init_state,
        local_width,
    )
    grad_gate_up, grad_down, grad_in_weight, grad_out_weight, result, grad_tokens = done[:6]
    grad_norm_gain, grad_mlp_gain, grad_mix_gain, grad_mix_bias, grad_rate, grad_init_state = done[6:]
    grad_gate_up = jnp.transpose(grad_gate_up, (2, 0, 1))
    return (
        result[None],
        grad_tokens[None],
        grad_norm_gain[0],
        grad_in_weight,
        grad_rate.T,
        grad_init_state,
        grad_mix_gain[0],
        grad_mix_bias[0],
        grad_out_weight,
        grad_mlp_gain[0],
        grad_gate_up,
        grad_down,
    )


def solution(mesh):
    square = mesh.shape["mlp"] == 4 and mesh.shape["head"] == 8
    return jax.shard_map(
        on_square if square else on_device,
        mesh=mesh,
        in_specs=(
            P("mlp", "head", None),
            P("mlp", "head", None),
            P("mlp", None),
            P(),
            P(None, None, "head"),
            P(None, "head"),
            P("head", None, None),
            P("head"),
            P("head"),
            P("head", None),
            P(),
            P(None, None, "mlp"),
            P("mlp", None),
        ),
        out_specs=(
            P("mlp", "head", None),
            P("mlp", "head", None),
            P(),
            P(None, None, "head"),
            P(None, "head"),
            P("head", None, None),
            P("head"),
            P("head"),
            P("head", None),
            P(),
            P(None, None, "mlp"),
            P("mlp", None),
        ),
        check_vma=False,
    )
```

time: 1660 us -> 452 us (0.27); the launches traced: 1630 us -> 451 us
  local copies, waits for them, and re-layouts: 512 us -> 0.01 us
  Pallas kernels: 0 us -> 433 us
  matrix products: 431 us -> 4.43 us
  waiting for transfers between devices: 323 us -> 0.04 us
  other arithmetic: 223 us -> 0 us
  loops' own time: 93.2 us -> 0 us
  blocking collectives: 32.9 us -> 0 us
    pallas_call x0 -> x8, Pallas kernels: none -> 433 us  [the longest x1 108 us: mlp_grads(): pl.pallas_call(grads_kernel, grid=(2,), in_specs=anywhere(len(arrays)) +...]
    dot_general x1098 -> x0, matrix products: 406 us -> none  [the longest x256 125 us: advance(): jnp.einsum('thi,hij->thj', key_rows, inner_state, precision=PRECISE)]
    squeeze x256 -> x0, local copies, waits for them, and re-layouts: 218 us -> none  [mixer(): lax.scan(jax.checkpoint(advance), zero_state, (split_rows, step_rates, re...]
    reduce_scatter x4 -> x0, waiting for transfers between devices: 125 us -> none  [the longest x1 48.2 us: on_device(): lax.psum_scatter(jnp.dot(mixed_part, out_weight, preferred_element_type=j...]
    dynamic_slice x256 -> x0, local copies, waits for them, and re-layouts: 124 us -> none  [mixer(): lax.scan(jax.checkpoint(advance), zero_state, (split_rows, step_rates, re...]
    all_gather x4 -> x1, waiting for transfers between devices: 117 us -> 0.02 us  [on_square(): lax.all_gather(after(d_branch, d_mixed), 'head', axis=0, tiled=True)]
    another operation x2 -> x0, loops' own time: 93.2 us -> none  [mixer(): lax.scan(jax.checkpoint(advance), zero_state, (split_rows, step_rates, re...]
    add x129 -> x0, other arithmetic: 85.2 us -> none  [the longest x128 85.2 us: advance(): inner_state = reset_flag * initial + (1.0 - reset_flag) * inner_state]
  transfers between devices with their start and end apart: 10 -> 1, of which waited for: 8 -> 0; matrix products, arithmetic and copies ran while one was open for 47% -> 0% of each run, Pallas kernels for 0% -> 13%
where the time goes in v1:
time: 452 us; the launch traced here: 451 us
  Pallas kernels  433 us (96%)
  between operations  14.1 us (3%)
    pallas_call x1, Pallas kernels, mlp_grads(): pl.pallas_call(grads_kernel, grid=(2,), in_specs=anywhere(len(arrays)) +...  108 us
    pallas_call x1, Pallas kernels, head(): pl.pallas_call(head_kernel, in_specs=[pl.BlockSpec(memory_space=pltpu.SME...  102 us
    pallas_call x1, Pallas kernels, spread_plane(): pl.pallas_call(spread_kernel, in_specs=[vmem, vmem, vmem, *anywhere(4)],...  45.7 us
    pallas_call x1, Pallas kernels, turn(): pl.pallas_call(turn_kernel, in_specs=anywhere(5) + [vmem] * 3, out_specs=...  45.5 us
    pallas_call x1, Pallas kernels, mlp_plane(): pl.pallas_call(carry.wrap(plane_kernel, 6, 5), grid=(hidden // PLANE_UNIT...  42.3 us
    pallas_call x1, Pallas kernels, mixer_backward(): pl.pallas_call(carry.wrap(backward_kernel, 11, 4), grid=(chunks,), in_spe...  37.1 us
    pallas_call x1, Pallas kernels, finish(): pl.pallas_call(finish_kernel, grid=(steps,), in_specs=[tile(2, FINISH, wi...  31.5 us
    pallas_call x1, Pallas kernels, dots(): pl.pallas_call(dots_kernel, grid=(width // SPAN,), in_specs=[full(*dproj....  21.1 us
  transfers between devices with their start and end apart: 1, of which 0 were waited for; matrix products, arithmetic and copies ran while one was open for 0% of the time, Pallas kernels for 13%

profile of v1, /device:TPU:0, one launch (start us, length us, event | category | flops | bytes accessed | tf_op | source)
XLA Modules:
  0.0 451.2 jit_solution(14599675892410536954)
XLA Ops:
  7.2 0.0 all-gather.2.cloned.1.call-start
  7.2 101.5 %head.1 = (f32[1024,1152]{1,0:T(8,128)}, bf16[128,2048]{1,0:T(8,128)(2,1)}, bf16[1024,256]{1,0:T(8,128)(2,1)}, bf16[1024,256]{1,0:T(8,128)(2,1)}, f32[1024,256]{...) custom-call(s32[1,6]{1,0:T(1,128)} %refs_0_.3, ...), custom_call_target="tpu_custom_call" | custom-call | flops 4294967296 | bytes 8388608 | tf_op jit(solution)/shard_map/head/pallas_call | solution.py:882
  108.8 45.7 %spread_plane.1 = (f32[128,2048]{1,0:T(8,128)}, bf16[128,2048]{1,0:T(8,128)(2,1)}, bf16[3,128,2048]{2,1,0:T(8,128)(2,1)}, bf16[192,2048]{1,0:T(8,128)(2,1)}, bf1...) custom-call(bf16[2,128,1024]{2,1,0:T(8,128)(2,1)} %get-tuple-element.88.refs_0_, bf16[128,2048]{1,0:T(8,128)(2,1)} %bitcast.29, ...), custom_call_target="tpu_custom_call" | custom-call | flops 1073741824 | bytes 12582912 | tf_op jit(solution)/shard_map/spread_plane/pallas_call | solution.py:1861
  154.5 42.3 %mlp_plane.1 = (bf16[4,128,2048]{2,1,0:T(8,128)(2,1)}, bf16[4,128,2048]{2,1,0:T(8,128)(2,1)}, bf16[1376,512]{1,0:T(8,128)(2,1)}, bf16[1376,512]{1,0:T(8,128)(2,1...) custom-call(bf16[128,2048]{1,0:T(8,128)(2,1)} %get-tuple-element.93., ...), custom_call_target="tpu_custom_call" | custom-call | flops 17314086912 | bytes 16908288 | tf_op jit(solution)/shard_map/mlp_plane/pallas_call | solution.py:1016
  196.8 45.5 %turn.1 = (bf16[1024,256]{1,0:T(8,128)(2,1)}, bf16[192,2048]{1,0:T(8,128)(2,1)}, f32[128,2048]{1,0:T(8,128)}, bf16[128,2048]{1,0:T(8,128)(2,1)}, f32[1,2048]{1,0:T(1,128)}, /*index=5*/f32[128,2048]{1,0:T(8,128)}) custom-call(bf16[4,128,2048]{2,1,0:T(8,128)(2,1)} %get-tuple-element.100.refs_0_, bf16[4,128,2048]{2,1,0:T(8,128)(2,1)} %get-tuple-element.101.refs_1_, ...), custom_call_target="tpu_custom_call" | custom-call | flops 1073741824 | bytes 16777216 | tf_op jit(solution)/shard_map/turn/pallas_call | solution.py:2014
  242.3 0.0 all-gather.2.cloned.1.call-update
  242.3 37.1 %mixer_backward.1 = (bf16[1024,1152]{1,0:T(8,128)(2,1)}, f32[4,64,64]{2,1,0:T(8,128)}, f32[1,256]{1,0:T(1,128)}, f32[1,256]{1,0:T(1,128)}, bf16[192,2048]{1,0:T(...) custom-call(s32[1,6]{1,0:T(1,128)} %refs_0_.3, ...), custom_call_target="tpu_custom_call" | custom-call | flops 1677721600 | bytes 10485760 | tf_op jit(solution)/shard_map/mixer_backward/pallas_call | solution.py:524
  279.4 0.0 copy-start
  279.4 21.1 %dots.1 = (bf16[2048,1024]{1,0:T(8,128)(2,1)}, bf16[1024,2048]{1,0:T(8,128)(2,1)}, f32[16,2048]{1,0:T(8,128)}, bf16[192,2048]{1,0:T(8,128)(2,1)}, bf16[192,2048]{1,0:T(8,128)(2,1)}) custom-call(bf16[1024,1152]{1,0:T(8,128)(2,1)} %get-tuple-element.115.refs_0_, bf16[1024,2048]{1,0:T(8,128)(2,1)} %get-tuple-element.116.refs_1_, ...), custom_call_target="tpu_custom_call" | custom-call | flops 9663676416 | bytes 25165824 | tf_op jit(solution)/shard_map/dots/pallas_call | solution.py:1447
  300.5 0.0 all-gather.2.cloned.1.call-done
  300.6 0.0 copy-done
  300.6 4.4 convolution_convert_fusion.refs_21_
  305.0 107.8 %mlp_grads.1 = (bf16[2,1376,2048]{2,1,0:T(8,128)(2,1)}, bf16[1376,2048]{1,0:T(8,128)(2,1)}, bf16[2,1376,2048]{2,1,0:T(8,128)(2,1)}, bf16[1376,2048]{1,0:T(8,128)...) custom-call(bf16[128,2048]{1,0:T(8,128)(2,1)} %get-tuple-element.93., ...), custom_call_target="tpu_custom_call" | custom-call | flops 63484985344 | bytes 39452672 | tf_op jit(solution)/shard_map/mlp_grads/pallas_call | solution.py:1364
  412.8 31.5 %finish.1 = (f32[2,1376,2048]{2,1,0:T(8,128)}, f32[1376,2048]{1,0:T(8,128)}, f32[2048,4,256]{2,1,0:T(4,128)}, f32[256,2048]{1,0:T(8,128)}, bf16[128,2048]{1,0:T(...) custom-call(bf16[2,1376,2048]{2,1,0:T(8,128)(2,1)} %get-tuple-elemen, ...), custom_call_target="tpu_custom_call" | custom-call | flops 8454144 | bytes 67633152 | tf_op jit(solution)/shard_map/finish/pallas_call | solution.py:1519
Async XLA Ops:
  7.2 293.4 %all-gather.2.cloned.1.call-start = ((), (), s32[]{:S(2)}) async-start(), calls=%async_computation | async-start | bytes 4718592 | tf_op jit(solution)/shard_map/all_gather | solution.py:2140
  279.4 21.2 %copy-start = (bf16[1024,256]{1,0:T(8,128)(2,1)S(1)}, bf16[1024,256]{1,0:T(8,128)(2,1)}, u32[]{:S(2)}) copy-start(bf16[1024,256]{1,0:T(8,128)(2,1)} %get-tuple-element.129) | copy-start | bytes 1572868
Sparse Core Ops, SparseCore 0:
  242.4 45.6 all-gather.1

commit v2 on v1

--- a/solution.py
+++ b/solution.py
@@ -634,7 +634,6 @@
             hop(chip, step).start()
 
     across(chip, core).start()
-    launch(out_moves, out_send, out_recv)
     launch(near_moves, near_send, near_recv)
     def product(of_chip):
         block = pl.ds(pl.multiple_of(of_chip * 2 * rows, 2 * rows), 2 * rows)
@@ -740,6 +739,7 @@
     outer = jnp.logical_not(inner)
     arrive(1)
     pl.when(inner)(lambda: arrive(2))
+    launch(out_moves, out_send, out_recv)
     load.wait()
     wide = raw.shape[2]
 

time: 452 us -> 452 us (level)
    pallas_call x1, Pallas kernels: 102 us -> 96.9 us  [head(): pl.pallas_call(head_kernel, in_specs=[pl.BlockSpec(memory_space=pltpu.SME...]
where the time goes in v2:
time: 452 us
  Pallas kernels  433 us (96%)
  between operations  14.1 us (3%)
    pallas_call x1, Pallas kernels, mlp_grads(): pl.pallas_call(grads_kernel, grid=(2,), in_specs=anywhere(len(arrays)) +...  108 us
    pallas_call x1, Pallas kernels, head(): pl.pallas_call(head_kernel, in_specs=[pl.BlockSpec(memory_space=pltpu.SME...  96.9 us
    pallas_call x1, Pallas kernels, spread_plane(): pl.pallas_call(spread_kernel, in_specs=[vmem, vmem, vmem, *anywhere(4)],...  49.9 us
    pallas_call x1, Pallas kernels, turn(): pl.pallas_call(turn_kernel, in_specs=anywhere(5) + [vmem] * 3, out_specs=...  45.6 us
    pallas_call x1, Pallas kernels, mlp_plane(): pl.pallas_call(carry.wrap(plane_kernel, 6, 5), grid=(hidden // PLANE_UNIT...  42.7 us
    pallas_call x1, Pallas kernels, mixer_backward(): pl.pallas_call(carry.wrap(backward_kernel, 11, 4), grid=(chunks,), in_spe...  37.1 us
    pallas_call x1, Pallas kernels, finish(): pl.pallas_call(finish_kernel, grid=(steps,), in_specs=[tile(2, FINISH, wi...  31.5 us
    pallas_call x1, Pallas kernels, dots(): pl.pallas_call(dots_kernel, grid=(width // SPAN,), in_specs=[full(*dproj....  21.1 us
  transfers between devices with their start and end apart: 1, of which 0 were waited for; matrix products, arithmetic and copies ran while one was open for 0% of the time, Pallas kernels for 13%

profile of v2, /device:TPU:0, one launch (start us, length us, event | category | flops | bytes accessed | tf_op | source)
XLA Modules:
  0.0 451.6 jit_solution(3358403974446319825)
XLA Ops:
  7.2 0.0 all-gather.2.cloned.1.call-start
  7.2 96.9 %head.1 = (f32[1024,1152]{1,0:T(8,128)}, bf16[128,2048]{1,0:T(8,128)(2,1)}, bf16[1024,256]{1,0:T(8,128)(2,1)}, bf16[1024,256]{1,0:T(8,128)(2,1)}, f32[1024,256]{...) custom-call(s32[1,6]{1,0:T(1,128)} %refs_0_.3, ...), custom_call_target="tpu_custom_call" | custom-call | flops 4294967296 | bytes 8388608 | tf_op jit(solution)/shard_map/head/pallas_call | solution.py:882
  104.2 49.9 %spread_plane.1 = (f32[128,2048]{1,0:T(8,128)}, bf16[128,2048]{1,0:T(8,128)(2,1)}, bf16[3,128,2048]{2,1,0:T(8,128)(2,1)}, bf16[192,2048]{1,0:T(8,128)(2,1)}, bf1...) custom-call(bf16[2,128,1024]{2,1,0:T(8,128)(2,1)} %get-tuple-element.88.refs_0_, bf16[128,2048]{1,0:T(8,128)(2,1)} %bitcast.29, ...), custom_call_target="tpu_custom_call" | custom-call | flops 1073741824 | bytes 12582912 | tf_op jit(solution)/shard_map/spread_plane/pallas_call | solution.py:1861
  154.1 42.7 %mlp_plane.1 = (bf16[4,128,2048]{2,1,0:T(8,128)(2,1)}, bf16[4,128,2048]{2,1,0:T(8,128)(2,1)}, bf16[1376,512]{1,0:T(8,128)(2,1)}, bf16[1376,512]{1,0:T(8,128)(2,1...) custom-call(bf16[128,2048]{1,0:T(8,128)(2,1)} %get-tuple-element.93., ...), custom_call_target="tpu_custom_call" | custom-call | flops 17314086912 | bytes 16908288 | tf_op jit(solution)/shard_map/mlp_plane/pallas_call | solution.py:1016
  196.9 45.6 %turn.1 = (bf16[1024,256]{1,0:T(8,128)(2,1)}, bf16[192,2048]{1,0:T(8,128)(2,1)}, f32[128,2048]{1,0:T(8,128)}, bf16[128,2048]{1,0:T(8,128)(2,1)}, f32[1,2048]{1,0:T(1,128)}, /*index=5*/f32[128,2048]{1,0:T(8,128)}) custom-call(bf16[4,128,2048]{2,1,0:T(8,128)(2,1)} %get-tuple-element.100.refs_0_, bf16[4,128,2048]{2,1,0:T(8,128)(2,1)} %get-tuple-element.101.refs_1_, ...), custom_call_target="tpu_custom_call" | custom-call | flops 1073741824 | bytes 16777216 | tf_op jit(solution)/shard_map/turn/pallas_call | solution.py:2014
  242.4 0.0 all-gather.2.cloned.1.call-update
  242.4 37.1 %mixer_backward.1 = (bf16[1024,1152]{1,0:T(8,128)(2,1)}, f32[4,64,64]{2,1,0:T(8,128)}, f32[1,256]{1,0:T(1,128)}, f32[1,256]{1,0:T(1,128)}, bf16[192,2048]{1,0:T(...) custom-call(s32[1,6]{1,0:T(1,128)} %refs_0_.3, ...), custom_call_target="tpu_custom_call" | custom-call | flops 1677721600 | bytes 10485760 | tf_op jit(solution)/shard_map/mixer_backward/pallas_call | solution.py:524
  279.5 0.0 copy-start
  279.5 21.1 %dots.1 = (bf16[2048,1024]{1,0:T(8,128)(2,1)}, bf16[1024,2048]{1,0:T(8,128)(2,1)}, f32[16,2048]{1,0:T(8,128)}, bf16[192,2048]{1,0:T(8,128)(2,1)}, bf16[192,2048]{1,0:T(8,128)(2,1)}) custom-call(bf16[1024,1152]{1,0:T(8,128)(2,1)} %get-tuple-element.115.refs_0_, bf16[1024,2048]{1,0:T(8,128)(2,1)} %get-tuple-element.116.refs_1_, ...), custom_call_target="tpu_custom_call" | custom-call | flops 9663676416 | bytes 25165824 | tf_op jit(solution)/shard_map/dots/pallas_call | solution.py:1447
  300.7 0.0 all-gather.2.cloned.1.call-done
  300.7 0.0 copy-done
  300.7 4.4 convolution_convert_fusion.refs_21_
  305.1 108.1 %mlp_grads.1 = (bf16[2,1376,2048]{2,1,0:T(8,128)(2,1)}, bf16[1376,2048]{1,0:T(8,128)(2,1)}, bf16[2,1376,2048]{2,1,0:T(8,128)(2,1)}, bf16[1376,2048]{1,0:T(8,128)...) custom-call(bf16[128,2048]{1,0:T(8,128)(2,1)} %get-tuple-element.93., ...), custom_call_target="tpu_custom_call" | custom-call | flops 63484985344 | bytes 39452672 | tf_op jit(solution)/shard_map/mlp_grads/pallas_call | solution.py:1364
  413.2 31.5 %finish.1 = (f32[2,1376,2048]{2,1,0:T(8,128)}, f32[1376,2048]{1,0:T(8,128)}, f32[2048,4,256]{2,1,0:T(4,128)}, f32[256,2048]{1,0:T(8,128)}, bf16[128,2048]{1,0:T(...) custom-call(bf16[2,1376,2048]{2,1,0:T(8,128)(2,1)} %get-tuple-elemen, ...), custom_call_target="tpu_custom_call" | custom-call | flops 8454144 | bytes 67633152 | tf_op jit(solution)/shard_map/finish/pallas_call | solution.py:1519
Async XLA Ops:
  7.2 293.5 %all-gather.2.cloned.1.call-start = ((), (), s32[]{:S(2)}) async-start(), calls=%async_computation | async-start | bytes 4718592 | tf_op jit(solution)/shard_map/all_gather | solution.py:2140
  279.5 21.2 %copy-start = (bf16[1024,256]{1,0:T(8,128)(2,1)S(1)}, bf16[1024,256]{1,0:T(8,128)(2,1)}, u32[]{:S(2)}) copy-start(bf16[1024,256]{1,0:T(8,128)(2,1)} %get-tuple-element.129) | copy-start | bytes 1572868
Sparse Core Ops, SparseCore 0:
  242.6 45.7 all-gather.1
